TPU v7x, 32 devices: a whole 2x2x4 slice. The times are simulated.
32 devices in a mesh: depth: 16 (over z, y, x), strip: 2 (over core).
Axes of the slice: x: 2, y: 2, z: 4, core: 2. Of those that a mesh axis runs over, the one named last changes fastest.
Arguments:
- volume: float32 [32, 128, 1024], P('strip', 'depth'), may hold values from -4.5 to 6.5
- extinction: float32 [1], replicated, may hold values from 0.00234375 to 0.0078125
- color_map: float32 [3, 2], replicated, may hold values from -3 to 3
- light_direction: float32 [3], replicated, may hold values from -4 to 4
Outputs:
- image: float32 [4, 32, 1024], P(None, 'strip', 'depth')
All inputs are finite; a program needn't handle non-finite values.
Results may differ from a plain program's by a relative error of at most 0.000034.
Values sent between devices are 32-bit elements; how exact they have to be, the bound alone decides.
A program may use at most 64 MiB of HBM per device.

v0:
```python
import jax
import jax.numpy as jnp
from jax import lax
from jax.sharding import PartitionSpec as P


def extended_2(block, sides, width):
    for axis, dim in sides:
        count = lax.axis_size(axis)
        forward = [(i, i + 1) for i in range(count - 1)]
        backward = [(target, source) for source, target in forward]
        low = lax.ppermute(
            lax.slice_in_dim(block, block.shape[dim] - width, None, axis=dim), axis, forward
        )
        high = lax.ppermute(lax.slice_in_dim(block, 0, width, axis=dim), axis, backward)
        block = jnp.concatenate([low, block, high], axis=dim)
    return block


def partner_2(value, axis, distance):
    mask = 2**distance
    pairs = [(source, source ^ mask) for source in range(lax.axis_size(axis))]
    return lax.ppermute(value, axis, pairs)


def blur_valid(field_in, along):
    extent = field_in.shape[along]
    lower_cells = lax.slice_in_dim(field_in, 0, extent - 2, axis=along)
    middle = lax.slice_in_dim(field_in, 1, extent - 1, axis=along)
    upper_cells = lax.slice_in_dim(field_in, 2, extent, axis=along)
    return 0.25 * lower_cells + 0.5 * middle + 0.25 * upper_cells


def slope_valid(field_in, along):
    extent = field_in.shape[along]
    lower_cells = lax.slice_in_dim(field_in, 0, extent - 2, axis=along)
    upper_cells = lax.slice_in_dim(field_in, 2, extent, axis=along)
    return 0.5 * (upper_cells - lower_cells)


def smooth_all(padded):
    return blur_valid(blur_valid(blur_valid(padded, 0), 1), 2)


def gradients(padded):
    first = blur_valid(blur_valid(slope_valid(padded, 0), 1), 2)
    second = blur_valid(blur_valid(slope_valid(padded, 1), 0), 2)
    third = blur_valid(blur_valid(slope_valid(padded, 2), 0), 1)
    return (first, second, third)


def pad_columns(field_in):
    return jnp.pad(field_in, ((0, 0), (0, 0), (1, 1)))


def render_slab(smoothed, gradient, extinction, color_map, light_direction):
    facing = (
        gradient[0] * light_direction[0]
        + gradient[1] * light_direction[1]
        + gradient[2] * light_direction[2]
    )
    shading = 0.3 + 0.7 * facing * facing / (1.0 + facing * facing)
    optical = extinction[0] * jax.nn.softplus(2.0 * smoothed)
    opacity = 1.0 - jnp.exp(-optical)
    prior_depth = jnp.cumsum(optical, axis=1) - optical
    weights = jnp.exp(-prior_depth) * opacity * shading
    colors = jnp.stack(
        [
            jnp.sum(
                weights * jax.nn.sigmoid(color_map[channel, 0] * smoothed + color_map[channel, 1]),
                axis=1,
            )
            for channel in range(3)
        ],
        0,
    )
    transmit = jnp.exp(-jnp.sum(optical, axis=1))
    return jnp.concatenate([colors, transmit[None]], 0)


def over_blend(front_half, back_half):
    return jnp.concatenate(
        [front_half[:3] + front_half[3:] * back_half[:3], front_half[3:] * back_half[3:]], 0
    )


def local(volume, extinction, color_map, light_direction):
    row_count, slab_count, column_count = volume.shape
    groups = lax.axis_size("depth")
    extended = extended_2(volume, (("depth", 1), ("strip", 0)), 1)
    smoothed = smooth_all(pad_columns(extended))
    filtered = extended_2(smoothed, (("depth", 1), ("strip", 0)), 1)
    gradient = gradients(pad_columns(filtered))
    partial_value = render_slab(smoothed, gradient, extinction, color_map, light_direction)
    block_width = column_count // groups
    holding = partial_value.reshape(4, row_count, groups, block_width)
    levels = groups.bit_length() - 1
    for level in range(levels):
        remain = holding.shape[2]
        halves = holding.reshape(4, row_count, remain // 2, 2, block_width)
        bit_value = lax.axis_index("depth") >> level & 1
        is_front = bit_value == 0
        kept_half = jnp.where(is_front, halves[:, :, :, 0], halves[:, :, :, 1])
        sent_half = jnp.where(is_front, halves[:, :, :, 1], halves[:, :, :, 0])
        partner = partner_2(sent_half, "depth", level)
        front_half = jnp.where(is_front, kept_half, partner)
        back_half = jnp.where(is_front, partner, kept_half)
        holding = over_blend(front_half, back_half)
    final_block = holding.reshape(4, row_count, block_width)
    colors = final_block[:3]
    transmit = final_block[3]
    return jnp.concatenate([colors, 1.0 - transmit[None]], 0)


def solution(mesh):
    in_specs = (P("strip", "depth", None), P(), P(), P())
    out_specs = P(None, "strip", "depth")
    return jax.shard_map(local, mesh=mesh, in_specs=in_specs, out_specs=out_specs, check_vma=False)
```

profile of v0, /device:TPU:0, one launch (start us, length us, event | category | flops | bytes accessed | tf_op | source)
XLA Modules:
  0.0 73.0 jit_solution(10278164004390565981)
XLA Ops:
  0.0 0.0 copy-start
  0.0 1.4 %fusion.46 = (f32[16,1,1024]{2,1,0:T(1,128)S(1)}, f32[16,1,1024]{2,1,0:T(1,128)S(1)}) fusion(f32[16,8,1024]{2,1,0:T(8,128)} %param.4), kind=kLoop, calls=%fused_computation.132 | loop fusion | bytes 262144 | tf_op jit(solution)/shard_map/slice | solution.py:13
  1.4 1.3 %collective-permute-start.1 = (f32[16,1,1024]{2,1,0:T(1,128)S(1)}, f32[16,1,1024]{2,1,0:T(1,128)S(1)}, u32[]{:S(2)}, u32[]{:S(2)}) collective-permute-start(f32[16,1,1024]{2,1,0:T(1,128)S(1)} %get-tuple-element.23), channel_id=1, source_target_pairs={{2,0},{4,2},{6,4},{8,6},{10,8},{12,10},{14,12},{16,14},{18,16},{20... | collective-permute-start | bytes 196616 | tf_op jit(solution)/shard_map/ppermute | solution.py:15
  2.7 5.5 %collective-permute-start = (f32[16,1,1024]{2,1,0:T(1,128)S(1)}, f32[16,1,1024]{2,1,0:T(1,128)S(1)}, u32[]{:S(2)}, u32[]{:S(2)}) collective-permute-start(f32[16,1,1024]{2,1,0:T(1,128)S(1)} %get-tuple-element.22), channel_id=1, source_target_pairs={{0,2},{2,4},{4,6},{6,8},{8,10},{10,12},{12,14},{14,16},{16,18},{18... | collective-permute-start | bytes 196616 | tf_op jit(solution)/shard_map/ppermute | solution.py:12
  8.2 0.3 collective-permute-done.1
  8.5 2.4 %collective-permute-done = f32[16,1,1024]{2,1,0:T(1,128)S(1)} collective-permute-done((f32[16,1,1024]{2,1,0:T(1,128)S(1)}, f32[16,1,1024]{2,1,0:T(1,128)S(1)}, u32[]{:S(2)}, u32[]{:S(2)}) %collective-permute-start) | collective-permute-done | bytes 65568 | tf_op jit(solution)/shard_map/ppermute | solution.py:12
  10.8 0.8 %pad_maximum_fusion.7 = (f32[1,10,1024]{2,1,0:T(8,128)S(1)}, f32[1,10,1024]{2,1,0:T(8,128)S(1)}) fusion(f32[16,1,1024]{2,1,0:T(1,128)S(1)} %collective-permute-done.1, f32[16,8,1024]{2,1,0:T(8,128)} %param.4, f32[16,1,1024]{2,1,0:T(1,128)S(1)} %collective-permute-done), kind=kLoop, calls=%fused_computation.95 | loop fusion | flops 40960 | bytes 737280 | tf_op jit(solution)/shard_map/slice | solution.py:13
  11.6 1.3 %collective-permute-start.3 = (f32[1,10,1024]{2,1,0:T(8,128)S(1)}, f32[1,10,1024]{2,1,0:T(8,128)S(1)}, u32[]{:S(2)}, u32[]{:S(2)}) collective-permute-start(f32[1,10,1024]{2,1,0:T(8,128)S(1)} %get-tuple-element.16), channel_id=1, source_target_pairs={{1,0},{3,2},{5,4},{7,6},{9,8},{11,10},{13,12},{15,14},{17,16},{19,... | collective-permute-start | bytes 122888 | tf_op jit(solution)/shard_map/ppermute | solution.py:15
  12.9 3.0 %collective-permute-start.2 = (f32[1,10,1024]{2,1,0:T(8,128)S(1)}, f32[1,10,1024]{2,1,0:T(8,128)S(1)}, u32[]{:S(2)}, u32[]{:S(2)}) collective-permute-start(f32[1,10,1024]{2,1,0:T(8,128)S(1)} %get-tuple-element.15), channel_id=1, source_target_pairs={{0,1},{2,3},{4,5},{6,7},{8,9},{10,11},{12,13},{14,15},{16,17},{18,... | collective-permute-start | bytes 122888 | tf_op jit(solution)/shard_map/ppermute | solution.py:12
  16.0 1.6 %fusion.47 = (f32[1,1]{0,1:T(1,128)}, f32[1,1]{0,1:T(1,128)}, f32[1,1]{0,1:T(1,128)}, f32[1,1]{0,1:T(1,128)}, f32[1,1]{0,1:T(1,128)}, /*index=5*/f32[1,1]{0,1:T(1,128)}) fusion(f32[3,2]{0,1:T(2,128)} %param.6), kind=kLoop, calls=%fused_computation.133 | loop fusion | bytes 48 | tf_op jit(solution)/shard_map/slice | solution.py:70
  18.2 0.0 collective-permute-done.3
  18.2 0.0 collective-permute-done.2
  18.2 0.0 copy-done
  18.2 0.7 select_maximum_fusion.4
  19.0 0.2 fusion.3
  19.1 0.2 fusion.12
  19.3 0.0 copy-start.1
  19.3 0.6 fusion.41
  20.0 0.1 fusion.45
  20.1 1.3 %collective-permute-start.5 = (f32[16,1,1024]{2,1,0:T(1,128)S(1)}, f32[16,1,1024]{2,1,0:T(1,128)S(1)}, u32[]{:S(2)}, u32[]{:S(2)}) collective-permute-start(f32[16,1,1024]{2,1,0:T(1,128)S(1)} %get-tuple-element.21), channel_id=1, source_target_pairs={{2,0},{4,2},{6,4},{8,6},{10,8},{12,10},{14,12},{16,14},{18,16},{20... | collective-permute-start | bytes 196616 | tf_op jit(solution)/shard_map/ppermute | solution.py:15
  21.4 5.0 %collective-permute-start.4 = (f32[16,1,1024]{2,1,0:T(1,128)S(1)}, f32[16,1,1024]{2,1,0:T(1,128)S(1)}, u32[]{:S(2)}, u32[]{:S(2)}) collective-permute-start(f32[16,1,1024]{2,1,0:T(1,128)S(1)} %get-tuple-element.20), channel_id=1, source_target_pairs={{0,2},{2,4},{4,6},{6,8},{8,10},{10,12},{12,14},{14,16},{16,18},{18... | collective-permute-start | bytes 196616 | tf_op jit(solution)/shard_map/ppermute | solution.py:12
  26.4 0.0 copy-done.1
  26.4 0.6 fusion.48
  27.0 0.0 collective-permute-done.5
  27.0 1.4 %collective-permute-done.4 = f32[16,1,1024]{2,1,0:T(1,128)S(1)} collective-permute-done((f32[16,1,1024]{2,1,0:T(1,128)S(1)}, f32[16,1,1024]{2,1,0:T(1,128)S(1)}, u32[]{:S(2)}, u32[]{:S(2)}) %collective-permute-start.4) | collective-permute-done | bytes 65568 | tf_op jit(solution)/shard_map/ppermute | solution.py:12
  28.5 1.3 %collective-permute-start.7 = (f32[1,10,1024]{2,1,0:T(8,128)S(1)}, f32[1,10,1024]{2,1,0:T(8,128)S(1)}, u32[]{:S(2)}, u32[]{:S(2)}) collective-permute-start(f32[1,10,1024]{2,1,0:T(8,128)S(1)} %get-tuple-element.14), channel_id=1, source_target_pairs={{1,0},{3,2},{5,4},{7,6},{9,8},{11,10},{13,12},{15,14},{17,16},{19,... | collective-permute-start | bytes 122888 | tf_op jit(solution)/shard_map/ppermute | solution.py:15
  29.8 3.0 %collective-permute-start.6 = (f32[1,10,1024]{2,1,0:T(8,128)S(1)}, f32[1,10,1024]{2,1,0:T(8,128)S(1)}, u32[]{:S(2)}, u32[]{:S(2)}) collective-permute-start(f32[1,10,1024]{2,1,0:T(8,128)S(1)} %get-tuple-element.13), channel_id=1, source_target_pairs={{0,1},{2,3},{4,5},{6,7},{8,9},{10,11},{12,13},{14,15},{16,17},{18,... | collective-permute-start | bytes 122888 | tf_op jit(solution)/shard_map/ppermute | solution.py:12
  32.9 0.1 exp.40
  33.0 0.5 reduce_window_sum.11
  33.5 0.0 collective-permute-done.7
  33.5 0.3 collective-permute-done.6
  33.7 0.7 select_maximum_fusion
  34.5 0.4 fusion.1
  34.8 0.1 fusion.7
  34.9 0.1 fusion.2
  35.0 0.1 fusion.5
  35.2 0.3 fusion.8
  35.5 7.1 %multiply_reduce_fusion = (f32[16,1024]{1,0:T(8,128)S(1)}, f32[16,1024]{1,0:T(8,128)S(1)}, f32[16,1024]{1,0:T(8,128)S(1)}) fusion(f32[16,8,1024]{2,1,0:T(8,128)S(1)} %get-tuple-element.10, f32[]{:T(128)} %bitcast.9, f32[]{:T(128)} %bitcast.8, f32[]{:T(128)} %bitcast.7, f32[]{:T(128)} %bitcast.6, f32[]{:T(128)} %bitcast.5, f32[]{:T(128)} %bitcast.4, ...), kind=kLoop, calls=%fused_computation.73 | loop fusion | flops 6897664 | bytes 6488100 | tf_op jit(solution)/shard_map/reduce_sum | solution.py:69
  42.6 0.1 concatenate.39
  42.7 0.1 concatenate.40
  42.8 0.1 concatenate.41
  43.1 0.5 fusion.44
  43.5 2.8 %collective-permute-start.8 = (f32[4,16,8,64]{3,2,1,0:T(8,128)S(1)}, f32[4,16,8,64]{3,2,1,0:T(8,128)S(1)}, u32[]{:S(2)}, u32[]{:S(2)}) collective-permute-start(f32[4,16,8,64]{3,2,1,0:T(8,128)S(1)} %bitcast.119), channel_id=1, source_target_pairs={{0,2},{2,0},{4,6},{6,4},{8,10},{10,8},{12,14},{14,12},{16,18},{18,... | collective-permute-start | bytes 393224 | tf_op jit(solution)/shard_map/ppermute | solution.py:23
  46.3 6.8 %collective-permute-done.8 = f32[4,16,8,64]{3,2,1,0:T(8,128)S(1)} collective-permute-done((f32[4,16,8,64]{3,2,1,0:T(8,128)S(1)}, f32[4,16,8,64]{3,2,1,0:T(8,128)S(1)}, u32[]{:S(2)}, u32[]{:S(2)}) %collective-permute-start.8) | collective-permute-done | bytes 131104 | tf_op jit(solution)/shard_map/ppermute | solution.py:23
  53.3 3.6 %collective-permute-start.9 = (f32[4,16,4,64]{3,1,2,0:T(8,128)S(1)}, f32[4,16,4,64]{3,1,2,0:T(8,128)S(1)}, u32[]{:S(2)}, u32[]{:S(2)}) collective-permute-start(f32[4,16,4,64]{3,1,2,0:T(8,128)S(1)} %select_bitcast_fusion), channel_id=1, source_target_pairs={{0,4},{2,6},{4,0},{6,2},{8,12},{10,14},{12,8},{14,10},{16,20},{18,... | collective-permute-start | bytes 196616 | tf_op jit(solution)/shard_map/ppermute | solution.py:23
  56.9 3.2 %collective-permute-done.9 = f32[4,16,4,64]{3,1,2,0:T(8,128)S(1)} collective-permute-done((f32[4,16,4,64]{3,1,2,0:T(8,128)S(1)}, f32[4,16,4,64]{3,1,2,0:T(8,128)S(1)}, u32[]{:S(2)}, u32[]{:S(2)}) %collective-permute-start.9) | collective-permute-done | bytes 65568 | tf_op jit(solution)/shard_map/ppermute | solution.py:23
  60.3 4.6 %collective-permute-start.10 = (f32[4,16,2,64]{3,1,2,0:T(8,128)S(1)}, f32[4,16,2,64]{3,1,2,0:T(8,128)S(1)}, u32[]{:S(2)}, u32[]{:S(2)}) collective-permute-start(f32[4,16,2,64]{3,1,2,0:T(8,128)S(1)} %select_bitcast_fusion.1), channel_id=1, source_target_pairs={{0,8},{2,10},{4,12},{6,14},{8,0},{10,2},{12,4},{14,6},{16,24},{18,... | collective-permute-start | bytes 98312 | tf_op jit(solution)/shard_map/ppermute | solution.py:23
  64.8 2.2 %collective-permute-done.10 = f32[4,16,2,64]{3,1,2,0:T(8,128)S(1)} collective-permute-done((f32[4,16,2,64]{3,1,2,0:T(8,128)S(1)}, f32[4,16,2,64]{3,1,2,0:T(8,128)S(1)}, u32[]{:S(2)}, u32[]{:S(2)}) %collective-permute-start.10) | collective-permute-done | bytes 32800 | tf_op jit(solution)/shard_map/ppermute | solution.py:23
  67.2 3.3 %collective-permute-start.11 = (f32[4,16,1,64]{3,1,0,2:T(8,128)S(1)}, f32[4,16,1,64]{3,1,0,2:T(8,128)S(1)}, u32[]{:S(2)}, u32[]{:S(2)}) collective-permute-start(f32[4,16,1,64]{3,1,0,2:T(8,128)S(1)} %select_bitcast_fusion.2), channel_id=1, source_target_pairs={{0,16},{2,18},{4,20},{6,22},{8,24},{10,26},{12,28},{14,30},{16,0},... | collective-permute-start | bytes 49160 | tf_op jit(solution)/shard_map/ppermute | solution.py:23
  70.5 1.9 %collective-permute-done.11 = f32[4,16,1,64]{3,1,0,2:T(8,128)S(1)} collective-permute-done((f32[4,16,1,64]{3,1,0,2:T(8,128)S(1)}, f32[4,16,1,64]{3,1,0,2:T(8,128)S(1)}, u32[]{:S(2)}, u32[]{:S(2)}) %collective-permute-start.11) | collective-permute-done | bytes 16416 | tf_op jit(solution)/shard_map/ppermute | solution.py:23
  72.4 0.6 pad_maximum_fusion.8
  (25 shorter events, 0.4 us)
Async XLA Ops:
  0.0 18.2 %copy-start = (f32[16,8,1024]{2,1,0:T(8,128)S(1)}, f32[16,8,1024]{2,1,0:T(8,128)}, u32[]{:S(2)}) copy-start(f32[16,8,1024]{2,1,0:T(8,128)} %param.4) | copy-start | bytes 1572868
  1.4 7.1 %collective-permute-start.1 = (f32[16,1,1024]{2,1,0:T(1,128)S(1)}, f32[16,1,1024]{2,1,0:T(1,128)S(1)}, u32[]{:S(2)}, u32[]{:S(2)}) collective-permute-start(f32[16,1,1024]{2,1,0:T(1,128)S(1)} %get-tuple-element.23), channel_id=1, source_target_pairs={{2,0},{4,2},{6,4},{8,6},{10,8},{12,10},{14,12},{16,14},{18,16},{20... | collective-permute-start | bytes 196616 | tf_op jit(solution)/shard_map/ppermute | solution.py:15
  2.7 8.1 %collective-permute-start = (f32[16,1,1024]{2,1,0:T(1,128)S(1)}, f32[16,1,1024]{2,1,0:T(1,128)S(1)}, u32[]{:S(2)}, u32[]{:S(2)}) collective-permute-start(f32[16,1,1024]{2,1,0:T(1,128)S(1)} %get-tuple-element.22), channel_id=1, source_target_pairs={{0,2},{2,4},{4,6},{6,8},{8,10},{10,12},{12,14},{14,16},{16,18},{18... | collective-permute-start | bytes 196616 | tf_op jit(solution)/shard_map/ppermute | solution.py:12
  11.6 6.6 %collective-permute-start.3 = (f32[1,10,1024]{2,1,0:T(8,128)S(1)}, f32[1,10,1024]{2,1,0:T(8,128)S(1)}, u32[]{:S(2)}, u32[]{:S(2)}) collective-permute-start(f32[1,10,1024]{2,1,0:T(8,128)S(1)} %get-tuple-element.16), channel_id=1, source_target_pairs={{1,0},{3,2},{5,4},{7,6},{9,8},{11,10},{13,12},{15,14},{17,16},{19,... | collective-permute-start | bytes 122888 | tf_op jit(solution)/shard_map/ppermute | solution.py:15
  12.9 5.3 %collective-permute-start.2 = (f32[1,10,1024]{2,1,0:T(8,128)S(1)}, f32[1,10,1024]{2,1,0:T(8,128)S(1)}, u32[]{:S(2)}, u32[]{:S(2)}) collective-permute-start(f32[1,10,1024]{2,1,0:T(8,128)S(1)} %get-tuple-element.15), channel_id=1, source_target_pairs={{0,1},{2,3},{4,5},{6,7},{8,9},{10,11},{12,13},{14,15},{16,17},{18,... | collective-permute-start | bytes 122888 | tf_op jit(solution)/shard_map/ppermute | solution.py:12
  19.3 7.1 %copy-start.1 = (f32[3]{0:T(128)S(1)}, f32[3]{0:T(128)}, u32[]{:S(2)}) copy-start(f32[3]{0:T(128)} %param.7) | copy-start | bytes 40
  20.1 7.0 %collective-permute-start.5 = (f32[16,1,1024]{2,1,0:T(1,128)S(1)}, f32[16,1,1024]{2,1,0:T(1,128)S(1)}, u32[]{:S(2)}, u32[]{:S(2)}) collective-permute-start(f32[16,1,1024]{2,1,0:T(1,128)S(1)} %get-tuple-element.21), channel_id=1, source_target_pairs={{2,0},{4,2},{6,4},{8,6},{10,8},{12,10},{14,12},{16,14},{18,16},{20... | collective-permute-start | bytes 196616 | tf_op jit(solution)/shard_map/ppermute | solution.py:15
  21.4 7.1 %collective-permute-start.4 = (f32[16,1,1024]{2,1,0:T(1,128)S(1)}, f32[16,1,1024]{2,1,0:T(1,128)S(1)}, u32[]{:S(2)}, u32[]{:S(2)}) collective-permute-start(f32[16,1,1024]{2,1,0:T(1,128)S(1)} %get-tuple-element.20), channel_id=1, source_target_pairs={{0,2},{2,4},{4,6},{6,8},{8,10},{10,12},{12,14},{14,16},{16,18},{18... | collective-permute-start | bytes 196616 | tf_op jit(solution)/shard_map/ppermute | solution.py:12
  28.5 5.0 %collective-permute-start.7 = (f32[1,10,1024]{2,1,0:T(8,128)S(1)}, f32[1,10,1024]{2,1,0:T(8,128)S(1)}, u32[]{:S(2)}, u32[]{:S(2)}) collective-permute-start(f32[1,10,1024]{2,1,0:T(8,128)S(1)} %get-tuple-element.14), channel_id=1, source_target_pairs={{1,0},{3,2},{5,4},{7,6},{9,8},{11,10},{13,12},{15,14},{17,16},{19,... | collective-permute-start | bytes 122888 | tf_op jit(solution)/shard_map/ppermute | solution.py:15
  29.8 3.9 %collective-permute-start.6 = (f32[1,10,1024]{2,1,0:T(8,128)S(1)}, f32[1,10,1024]{2,1,0:T(8,128)S(1)}, u32[]{:S(2)}, u32[]{:S(2)}) collective-permute-start(f32[1,10,1024]{2,1,0:T(8,128)S(1)} %get-tuple-element.13), channel_id=1, source_target_pairs={{0,1},{2,3},{4,5},{6,7},{8,9},{10,11},{12,13},{14,15},{16,17},{18,... | collective-permute-start | bytes 122888 | tf_op jit(solution)/shard_map/ppermute | solution.py:12
  43.5 9.6 %collective-permute-start.8 = (f32[4,16,8,64]{3,2,1,0:T(8,128)S(1)}, f32[4,16,8,64]{3,2,1,0:T(8,128)S(1)}, u32[]{:S(2)}, u32[]{:S(2)}) collective-permute-start(f32[4,16,8,64]{3,2,1,0:T(8,128)S(1)} %bitcast.119), channel_id=1, source_target_pairs={{0,2},{2,0},{4,6},{6,4},{8,10},{10,8},{12,14},{14,12},{16,18},{18,... | collective-permute-start | bytes 393224 | tf_op jit(solution)/shard_map/ppermute | solution.py:23
  53.3 6.8 %collective-permute-start.9 = (f32[4,16,4,64]{3,1,2,0:T(8,128)S(1)}, f32[4,16,4,64]{3,1,2,0:T(8,128)S(1)}, u32[]{:S(2)}, u32[]{:S(2)}) collective-permute-start(f32[4,16,4,64]{3,1,2,0:T(8,128)S(1)} %select_bitcast_fusion), channel_id=1, source_target_pairs={{0,4},{2,6},{4,0},{6,2},{8,12},{10,14},{12,8},{14,10},{16,20},{18,... | collective-permute-start | bytes 196616 | tf_op jit(solution)/shard_map/ppermute | solution.py:23
  60.3 6.8 %collective-permute-start.10 = (f32[4,16,2,64]{3,1,2,0:T(8,128)S(1)}, f32[4,16,2,64]{3,1,2,0:T(8,128)S(1)}, u32[]{:S(2)}, u32[]{:S(2)}) collective-permute-start(f32[4,16,2,64]{3,1,2,0:T(8,128)S(1)} %select_bitcast_fusion.1), channel_id=1, source_target_pairs={{0,8},{2,10},{4,12},{6,14},{8,0},{10,2},{12,4},{14,6},{16,24},{18,... | collective-permute-start | bytes 98312 | tf_op jit(solution)/shard_map/ppermute | solution.py:23
  67.2 5.2 %collective-permute-start.11 = (f32[4,16,1,64]{3,1,0,2:T(8,128)S(1)}, f32[4,16,1,64]{3,1,0,2:T(8,128)S(1)}, u32[]{:S(2)}, u32[]{:S(2)}) collective-permute-start(f32[4,16,1,64]{3,1,0,2:T(8,128)S(1)} %select_bitcast_fusion.2), channel_id=1, source_target_pairs={{0,16},{2,18},{4,20},{6,22},{8,24},{10,26},{12,28},{14,30},{16,0},... | collective-permute-start | bytes 49160 | tf_op jit(solution)/shard_map/ppermute | solution.py:23
where the time goes:
time: 73.5 us; the launch traced here: 73 us
  starting transfers between devices  35.9 us (49%)
  waiting for transfers between devices  18.5 us (25%)
  other arithmetic  13.1 us (18%)
  local copies, waits for them, and re-layouts  4.32 us (6%)
  between operations  1.06 us (1%)
    ppermute x4, starting transfers between devices, extended_2(): lax.ppermute(lax.slice_in_dim(block, block.shape[dim] - width, None, axis...  16.6 us
    ppermute x4, starting transfers between devices, partner_2(): return lax.ppermute(value, axis, pairs)  14.2 us
    ppermute x4, waiting for transfers between devices, partner_2(): return lax.ppermute(value, axis, pairs)  14.2 us
    reduce_sum x1, other arithmetic, render_slab(): jnp.sum(weights * jax.nn.sigmoid(color_map[channel, 0] * smoothed + color...  7.1 us
    ppermute x4, starting transfers between devices, extended_2(): lax.ppermute(lax.slice_in_dim(block, 0, width, axis=dim), axis, backward)  5.17 us
    ppermute x4, waiting for transfers between devices, extended_2(): lax.ppermute(lax.slice_in_dim(block, block.shape[dim] - width, None, axis...  4.05 us
    slice x1, local copies, waits for them, and re-layouts, render_slab(): color_map[channel, 0] * smoothed + color_map[channel, 1]  1.57 us
  transfers between devices with their start and end apart: 12, of which 8 were waited for; matrix products, arithmetic and copies ran while one was open for 4% of the time, Pallas kernels for 0%

commit v1 on v0

v1 whole, which is shorter than its diff:
```python
import functools

import jax
import jax.numpy as jnp
from jax import lax
from jax.experimental import pallas as pl
from jax.experimental.pallas import tpu as pltpu
from jax.sharding import PartitionSpec as P

LANES = 128
EDGE = 8
MESH = pl.DeviceIdType.MESH
SIDES = [(dz, ds) for dz in (-1, 0, 1) for ds in (-1, 0, 1) if (dz, ds) != (0, 0)]


def radices_of(count):
    found = []
    while count > 1:
        radix = 4 if count % 4 == 0 else 2
        found.append(radix)
        count //= radix
    return found


def next_lane(here, after, lane):
    return pltpu.roll(jnp.where(lane == 0, after, here), LANES - 1, here.ndim - 1)


def previous_lane(here, before, lane):
    return pltpu.roll(jnp.where(lane == LANES - 1, before, here), 1, here.ndim - 1)


def place(parts, lane):
    result = None
    for tile, source, target, width in parts:
        shift = (target - source) % LANES
        moved = pltpu.roll(tile, shift, 1) if shift else tile
        if result is None:
            result = moved
        else:
            result = jnp.where((lane >= target) & (lane < target + width), moved, result)
    return result


def plan(groups, columns):
    levels, stride, held = [], 1, columns
    for radix in radices_of(groups):
        levels.append((radix, stride, held, held // radix))
        stride *= radix
        held //= radix
    return levels


def piece_tiles(width):
    if width >= LANES:
        return 1, 4 * (width // LANES)
    per = min(4, LANES // width)
    return per, -(-4 // per)


def kernel(groups, strips, rows, slabs, columns,
           ext_ref, color_ref, light_ref, vol_ref, out_ref,
           vol, ext_field, smooth, ahead, behind, picture, *rest):
    levels = plan(groups, columns)
    sent = rest[:len(levels)]
    got = rest[len(levels):2 * len(levels)]
    load_sem, halo_send, halo_recv, swap_send, swap_recv = rest[2 * len(levels):]
    tiles = columns // LANES
    block = columns // groups
    depth, strip = lax.axis_index("depth"), lax.axis_index("strip")
    lane = lax.broadcasted_iota(jnp.int32, (rows, LANES), 1)
    lane8 = lax.broadcasted_iota(jnp.int32, (8, LANES), 1)
    tall = rows + 8

    loads = [
        pltpu.make_async_copy(vol_ref.at[:, pl.ds(t * LANES, LANES)], vol.at[t], load_sem.at[t])
        for t in range(tiles)
    ]
    for load in loads:
        load.start()

    def there(dz, ds):
        return (depth + dz >= 0) & (depth + dz < groups) & (strip + ds >= 0) & (strip + ds < strips)

    def partner(level, step):
        radix, stride, _, _ = levels[level]
        digit = depth // stride % radix
        other = (digit + step) % radix
        return digit, other, depth + (other - digit) * stride

    barrier = pltpu.get_barrier_semaphore()
    expected = 0
    for dz, ds in SIDES:
        expected = expected + jnp.where(there(dz, ds), 1, 0)

        @pl.when(there(dz, ds))
        def _(dz=dz, ds=ds):
            pl.semaphore_signal(barrier, inc=1, device_id=(depth + dz, strip + ds), device_id_type=MESH)

    for level, (radix, _, _, _) in enumerate(levels):
        for step in range(1, radix):
            pl.semaphore_signal(
                barrier, inc=1, device_id=(partner(level, step)[2], strip), device_id_type=MESH
            )
            expected = expected + 1

    @pl.when(depth == 0)
    def _():
        ext_field[:, 0:2] = jnp.zeros((tiles, 2, rows + 2 * EDGE, LANES), jnp.float32)

    @pl.when(depth == groups - 1)
    def _():
        ext_field[:, slabs + 2:] = jnp.zeros((tiles, 2, rows + 2 * EDGE, LANES), jnp.float32)

    @pl.when(strip == 0)
    def _():
        ext_field[:, :, 0:EDGE] = jnp.zeros((tiles, slabs + 4, EDGE, LANES), jnp.float32)

    @pl.when(strip == strips - 1)
    def _():
        ext_field[:, :, rows + EDGE:] = jnp.zeros((tiles, slabs + 4, EDGE, LANES), jnp.float32)

    ahead[tiles] = jnp.zeros((slabs, rows, LANES), jnp.float32)
    behind[0] = jnp.zeros((slabs, rows, LANES), jnp.float32)

    for load in loads:
        load.wait()

    def blur_columns(z, carry):
        for h in range(rows // 8):
            cells = [vol[t, pl.ds(8 * h * slabs + z, 8, stride=slabs), :] for t in range(tiles)]
            nothing = jnp.zeros_like(cells[0])
            for t in range(tiles):
                before = cells[t - 1] if t > 0 else nothing
                after = cells[t + 1] if t < tiles - 1 else nothing
                ext_field[t, z + 2, EDGE + 8 * h:EDGE + 8 * h + 8] = (
                    next_lane(cells[t], after, lane8)
                    + previous_lane(cells[t], before, lane8)
                    + 2.0 * cells[t]
                )
        return carry

    lax.fori_loop(0, slabs, blur_columns, 0)
    pl.semaphore_wait(barrier, expected)

    first = levels[0]
    stages = max(1, first[3] // LANES)
    per_stage = tiles // stages
    ends = [min(tiles, (c + 1) * per_stage + 1) for c in range(stages)]
    starts = [0] + ends[:-1]

    def halo(c, index, sender):
        dz, ds = SIDES[index]
        span = pl.ds(starts[c], ends[c] - starts[c])
        z_from, z_to, z_count = {
            -1: (2, slabs + 2, 2), 0: (2, 2, slabs), 1: (slabs, 0, 2)}[dz]
        r_from, r_to, r_count = {
            -1: (EDGE, EDGE + rows, 2), 0: (EDGE, EDGE, rows), 1: (EDGE + rows - 2, EDGE - 2, 2)}[ds]
        sign = 1 if sender else -1
        return pltpu.make_async_remote_copy(
            src_ref=ext_field.at[span, pl.ds(z_from, z_count), pl.ds(r_from, r_count)],
            dst_ref=ext_field.at[span, pl.ds(z_to, z_count), pl.ds(r_to, r_count)],
            send_sem=halo_send.at[c, index],
            recv_sem=halo_recv.at[c, index],
            device_id=(depth + sign * dz, strip + sign * ds),
            device_id_type=MESH,
        )

    for c in range(stages):
        for index, (dz, ds) in enumerate(SIDES):
            @pl.when(there(dz, ds))
            def _(c=c, index=index):
                halo(c, index, True).start()

    row = lax.broadcasted_iota(jnp.int32, (tall, LANES), 0)
    inside = ((row > 0) | (strip > 0)) & ((row != rows + 1) | (strip < strips - 1))
    scale = jnp.where(inside, 1.0 / 64.0, 0.0)
    scale_front = jnp.where(inside & (depth > 0), 1.0 / 64.0, 0.0)
    scale_back = jnp.where(inside & (depth < groups - 1), 1.0 / 64.0, 0.0)
    light = [light_ref[0] / 32.0, light_ref[1] / 32.0, light_ref[2] / 32.0]

    def gradients(t, carry):
        def over_rows(z):
            return (
                ext_field[t, z, EDGE - 2:EDGE - 2 + tall]
                + ext_field[t, z, EDGE:EDGE + tall]
                + 2.0 * ext_field[t, z, EDGE - 1:EDGE - 1 + tall]
            )

        one, two = over_rows(0), over_rows(1)
        for z in range(slabs + 2):
            three = over_rows(z + 2)
            weight = scale_front if z == 0 else scale_back if z == slabs + 1 else scale
            smooth[t, z] = jnp.where(weight > 0.0, (one + three + 2.0 * two) * weight, 0.0)
            one, two = two, three

        def rows_of(z):
            low = smooth[t, z, 0:rows]
            middle = smooth[t, z, 1:rows + 1]
            high = smooth[t, z, 2:rows + 2]
            return low + high + 2.0 * middle, high - low

        sums, slopes = zip(*[rows_of(0), rows_of(1)])
        sums, slopes = list(sums), list(slopes)
        for z in range(slabs):
            more, steeper = rows_of(z + 2)
            sums.append(more)
            slopes.append(steeper)
            across = (
                light[0] * (slopes[z] + slopes[z + 2] + 2.0 * slopes[z + 1])
                + light[1] * (sums[z + 2] - sums[z])
            )
            along = light[2] * (sums[z] + sums[z + 2] + 2.0 * sums[z + 1])
            ahead[t, z] = across + along
            behind[t + 1, z] = across - along
        return carry

    extinction = ext_ref[0]
    slope = [0.5 * color_ref[k, 0] for k in range(3)]
    offset = [0.5 * color_ref[k, 1] for k in range(3)]

    def render(t, carry):
        optical = jnp.zeros((rows, LANES), jnp.float32)
        passed = jnp.ones((rows, LANES), jnp.float32)
        total = jnp.zeros((rows, LANES), jnp.float32)
        tinted = [jnp.zeros((rows, LANES), jnp.float32) for _ in range(3)]
        for z in range(slabs):
            up, down = ahead[t, z], behind[t + 1, z]
            facing = (
                next_lane(up, ahead[t + 1, z], lane)
                + previous_lane(down, behind[t, z], lane)
                + (up + down)
            )
            shading = 1.0 - 0.7 * pl.reciprocal(1.0 + facing * facing)
            field = smooth[t, z + 1, 1:rows + 1]
            double = 2.0 * field
            optical += extinction * (
                jnp.maximum(double, 0.0) + jnp.log1p(jnp.exp(-jnp.abs(double)))
            )
            beyond = jnp.exp(-optical)
            weight = (passed - beyond) * shading
            passed = beyond
            total += weight
            for k in range(3):
                tinted[k] += weight * jnp.tanh(slope[k] * field + offset[k])
        for k in range(3):
            picture[t, k] = 0.5 * (total + tinted[k])
        picture[t, 3] = passed
        return carry

    def swap(level, step, part, sender):
        digit, other, target = partner(level, step if sender else -step)
        source, slot = (other, digit) if sender else (digit, other)
        return pltpu.make_async_remote_copy(
            src_ref=sent[level].at[source, part],
            dst_ref=got[level].at[slot, part],
            send_sem=swap_send.at[level, step - 1, part],
            recv_sem=swap_recv.at[level, step - 1, part],
            device_id=(target, strip),
            device_id_type=MESH,
        )

    def dispatch(level, part):
        radix = levels[level][0]
        for step in range(1, radix):
            swap(level, step, part, True).start()
        digit = partner(level, 1)[0]
        got[level][digit, part] = sent[level][digit, part]

    def fill(level, part, tile_of):
        radix, _, held, width = levels[level]
        per, count = piece_tiles(width)
        for j in range(radix):
            blocks = [q * radix + j for q in range(width // block)]
            if width >= LANES:
                each = LANES // block
                blocks = blocks[part * each:(part + 1) * each]
                for k in range(4):
                    sent[level][j, part, k] = place(
                        [
                            (tile_of(k, b * block // LANES), b * block % LANES, i * block, block)
                            for i, b in enumerate(blocks)
                        ],
                        lane,
                    )
            else:
                for c in range(count):
                    sent[level][j, part, c] = place(
                        [
                            (
                                tile_of(k, b * block // LANES), b * block % LANES,
                                (k - c * per) * width + i * block, block,
                            )
                            for k in range(c * per, min(4, (c + 1) * per))
                            for i, b in enumerate(blocks)
                        ],
                        lane,
                    )

    for c in range(stages):
        for index, (dz, ds) in enumerate(SIDES):
            @pl.when(there(-dz, -ds))
            def _(c=c, index=index):
                halo(c, index, False).wait_recv()

        lax.fori_loop(starts[c], ends[c], gradients, 0)
        lax.fori_loop(c * per_stage, (c + 1) * per_stage, render, 0)
        fill(0, c, lambda k, t: picture[t, k])
        dispatch(0, c)

    current = None
    for level, (radix, _, held, width) in enumerate(levels):
        parts = max(1, width // LANES)
        if level > 0:
            for part in range(parts):
                fill(level, part, lambda k, t: current[t][k])
                dispatch(level, part)
        per, _ = piece_tiles(width)
        merged = []
        for part in range(parts):
            for step in range(1, radix):
                swap(level, step, part, False).wait_recv()

            def channel(j, k):
                tile = got[level][j, part, k // per]
                shift = -(k % per) * width % LANES
                return pltpu.roll(tile, shift, 1) if shift else tile

            value = [channel(0, k) for k in range(4)]
            for j in range(1, radix):
                value = [value[k] + value[3] * channel(j, k) for k in range(3)] + [
                    value[3] * channel(j, 3)
                ]
            merged.append(value)
        current = merged

    for k in range(4):
        out_ref[k] = current[0][k][:, :block]

    for c in range(stages):
        for index, (dz, ds) in enumerate(SIDES):
            @pl.when(there(dz, ds))
            def _(c=c, index=index):
                halo(c, index, True).wait_send()
    for level, (radix, _, _, width) in enumerate(levels):
        for part in range(max(1, width // LANES)):
            for step in range(1, radix):
                swap(level, step, part, True).wait_send()


def local(volume, extinction, color_map, light_direction):
    rows, slabs, columns = volume.shape
    groups, strips = lax.axis_size("depth"), lax.axis_size("strip")
    tiles, block = columns // LANES, columns // groups
    levels = plan(groups, columns)
    stages = max(1, levels[0][3] // LANES)
    f32 = jnp.float32
    buffers = []
    for radix, _, _, width in levels:
        parts = max(1, width // LANES)
        buffers.append(pltpu.VMEM((radix, parts, piece_tiles(width)[1] // parts, rows, LANES), f32))
    most = max(max(1, width // LANES) for _, _, _, width in levels)
    image = pl.pallas_call(
        functools.partial(kernel, groups, strips, rows, slabs, columns),
        out_shape=jax.ShapeDtypeStruct((4, rows, block), f32),
        in_specs=[pl.BlockSpec(memory_space=pltpu.SMEM)] * 3 + [pl.BlockSpec(memory_space=pl.ANY)],
        out_specs=pl.BlockSpec(memory_space=pltpu.VMEM),
        scratch_shapes=[
            pltpu.VMEM((tiles, rows * slabs, LANES), f32),
            pltpu.VMEM((tiles, slabs + 4, rows + 2 * EDGE, LANES), f32),
            pltpu.VMEM((tiles, slabs + 2, rows + 8, LANES), f32),
            pltpu.VMEM((tiles + 1, slabs, rows, LANES), f32),
            pltpu.VMEM((tiles + 1, slabs, rows, LANES), f32),
            pltpu.VMEM((tiles, 4, rows, LANES), f32),
            *buffers,
            *buffers,
            pltpu.SemaphoreType.DMA((tiles,)),
            pltpu.SemaphoreType.DMA((stages, len(SIDES))),
            pltpu.SemaphoreType.DMA((stages, len(SIDES))),
            pltpu.SemaphoreType.DMA((len(levels), 3, most)),
            pltpu.SemaphoreType.DMA((len(levels), 3, most)),
        ],
        compiler_params=pltpu.CompilerParams(
            collective_id=0, has_side_effects=True, vmem_limit_bytes=32 * 1024 * 1024
        ),
    )(extinction, color_map, light_direction, volume.reshape(rows * slabs, columns))
    last = lax.broadcasted_iota(jnp.int32, image.shape, 0) == 3
    return jnp.where(last, 1.0 - image, image)


def solution(mesh):
    in_specs = (P("strip", "depth", None), P(), P(), P())
    out_specs = P(None, "strip", "depth")
    return jax.shard_map(local, mesh=mesh, in_specs=in_specs, out_specs=out_specs, check_vma=False)
```

time: 73.5 us -> 27.3 us (0.37)
  starting transfers between devices: 35.9 us -> 0 us
  Pallas kernels: 0 us -> 23.3 us
  waiting for transfers between devices: 18.5 us -> 0 us
  other arithmetic: 13.1 us -> 0.69 us
  local copies, waits for them, and re-layouts: 4.32 us -> 2.46 us
    ppermute x12 -> x0, starting transfers between devices: 35.9 us -> none  [the longest x4 16.6 us: extended_2(): lax.ppermute(lax.slice_in_dim(block, block.shape[dim] - width, None, axis...]
    pallas_call x0 -> x1, Pallas kernels: none -> 23.3 us  [local(): pl.pallas_call(functools.partial(kernel, groups, strips, rows, slabs, col...]
    ppermute x12 -> x0, waiting for transfers between devices: 18.5 us -> none  [the longest x4 14.2 us: partner_2(): return lax.ppermute(value, axis, pairs)]
    reduce_sum x2 -> x0, other arithmetic: 7.73 us -> none  [the longest x1 7.1 us: render_slab(): jnp.sum(weights * jax.nn.sigmoid(color_map[channel, 0] * smoothed + color...]
    slice x4 -> x0, local copies, waits for them, and re-layouts: 3.68 us -> none  [the longest x1 1.57 us: render_slab(): color_map[channel, 0] * smoothed + color_map[channel, 1]]
    unnamed x7 -> x5, local copies, waits for them, and re-layouts: 0.06 us -> 2.46 us
    concatenate x5 -> x0, other arithmetic: 2.09 us -> none  [the longest x2 1.44 us: extended_2(): block = jnp.concatenate([low, block, high], axis=dim)]
    slice x4 -> x0, other arithmetic: 1.31 us -> none  [the longest x2 0.83 us: extended_2(): lax.slice_in_dim(block, block.shape[dim] - width, None, axis=dim)]
  transfers between devices with their start and end apart: 12 -> 0, of which waited for: 8 -> 0; matrix products, arithmetic and copies ran while one was open for 4% -> 0% of each run, Pallas kernels for 0% -> 0%
where the time goes in v1:
time: 27.3 us; the launch traced here: 27.1 us
  Pallas kernels  23.3 us (85%)
  local copies, waits for them, and re-layouts  2.46 us (9%)
  other arithmetic  0.69 us (3%)
  between operations  0.68 us (2%)
    pallas_call x1, Pallas kernels, local(): pl.pallas_call(functools.partial(kernel, groups, strips, rows, slabs, col...  23.3 us
    unnamed x5, local copies, waits for them, and re-layouts  2.46 us
    select_n x1, other arithmetic, local(): return jnp.where(last, 1.0 - image, image)  0.69 us

profile of v1, /device:TPU:0, one launch (start us, length us, event | category | flops | bytes accessed | tf_op | source)
XLA Modules:
  0.0 27.1 jit_solution(7195287722017640466)
XLA Ops:
  0.0 0.8 %copy.5.color_ref = f32[3,2]{1,0:T(4,128)S(1)} copy(f32[3,2]{0,1:T(2,128)} %param.6) | data formatting | bytes 48 | tf_op args[2]
  1.4 0.0 copy-start.1
  1.4 0.6 %copy-done.1 = f32[3]{0:T(128)S(1)} copy-done((f32[3]{0:T(128)S(1)}, f32[3]{0:T(128)}, u32[]{:S(2)}) %copy-start.1) | copy-done | bytes 36
  2.1 0.0 copy-start
  2.1 1.0 %copy-done = f32[16,8,1024]{2,1,0:T(8,128)S(1)} copy-done((f32[16,8,1024]{2,1,0:T(8,128)S(1)}, f32[16,8,1024]{2,1,0:T(8,128)}, u32[]{:S(2)}) %copy-start) | copy-done | bytes 524312
  3.1 23.3 %shard_map.46 = f32[4,16,64]{2,1,0:T(8,128)S(1)} custom-call(f32[1]{0:T(128)S(6)} %copy.6.ext_ref, f32[3,2]{1,0:T(4,128)S(1)} %copy.5.color_ref, f32[3]{0:T(128)S(1)} %copy-done.1, f32[128,1024]{1,0:T(8,128)S(1)} %bitcast.1), custom_call_target="tpu_custom_call" | custom-call | tf_op jit(solution)/shard_map/pallas_call | solution.py:363
  26.4 0.7 %subtract_select_fusion = f32[4,16,64]{2,1,0:T(8,128)} fusion(f32[4,16,64]{2,1,0:T(8,128)S(1)} %shard_map.46, pred[4]{0:T(512)(128)(4,1)S(1)} %iota_compare_fusion), kind=kLoop, calls=%fused_computation | loop fusion | flops 8192 | bytes 32772 | tf_op jit(solution)/shard_map/jit(_where)/select_n | solution.py:388
  (1 shorter events, 0.0 us)
Async XLA Ops:
  1.4 0.7 %copy-start.1 = (f32[3]{0:T(128)S(1)}, f32[3]{0:T(128)}, u32[]{:S(2)}) copy-start(f32[3]{0:T(128)} %light_ref.1) | copy-start | bytes 40
  2.1 1.0 %copy-start = (f32[16,8,1024]{2,1,0:T(8,128)S(1)}, f32[16,8,1024]{2,1,0:T(8,128)}, u32[]{:S(2)}) copy-start(f32[16,8,1024]{2,1,0:T(8,128)} %param.4) | copy-start | bytes 1572868

commit v2 on v1

--- a/solution.py
+++ b/solution.py
@@ -59,12 +59,12 @@
 
 
 def kernel(groups, strips, rows, slabs, columns,
-           ext_ref, color_ref, light_ref, vol_ref, out_ref,
-           vol, ext_field, smooth, ahead, behind, picture, *rest):
+           ext_hbm, color_hbm, light_hbm, vol_ref, out_ref,
+           ext_ref, color_ref, light_ref, vol, ext_field, smooth, ahead, behind, picture, *rest):
     levels = plan(groups, columns)
     sent = rest[:len(levels)]
     got = rest[len(levels):2 * len(levels)]
-    load_sem, halo_send, halo_recv, swap_send, swap_recv = rest[2 * len(levels):]
+    load_sem, small_sem, halo_send, halo_recv, swap_send, swap_recv = rest[2 * len(levels):]
     tiles = columns // LANES
     block = columns // groups
     depth, strip = lax.axis_index("depth"), lax.axis_index("strip")
@@ -78,6 +78,13 @@
     ]
     for load in loads:
         load.start()
+    scalars = [
+        pltpu.make_async_copy(source, target, small_sem.at[i])
+        for i, (source, target) in enumerate(
+            [(ext_hbm, ext_ref), (color_hbm, color_ref), (light_hbm, light_ref)])
+    ]
+    for scalar in scalars:
+        scalar.start()
 
     def there(dz, ds):
         return (depth + dz >= 0) & (depth + dz < groups) & (strip + ds >= 0) & (strip + ds < strips)
@@ -125,23 +132,6 @@
 
     for load in loads:
         load.wait()
-
-    def blur_columns(z, carry):
-        for h in range(rows // 8):
-            cells = [vol[t, pl.ds(8 * h * slabs + z, 8, stride=slabs), :] for t in range(tiles)]
-            nothing = jnp.zeros_like(cells[0])
-            for t in range(tiles):
-                before = cells[t - 1] if t > 0 else nothing
-                after = cells[t + 1] if t < tiles - 1 else nothing
-                ext_field[t, z + 2, EDGE + 8 * h:EDGE + 8 * h + 8] = (
-                    next_lane(cells[t], after, lane8)
-                    + previous_lane(cells[t], before, lane8)
-                    + 2.0 * cells[t]
-                )
-        return carry
-
-    lax.fori_loop(0, slabs, blur_columns, 0)
-    pl.semaphore_wait(barrier, expected)
 
     first = levels[0]
     stages = max(1, first[3] // LANES)
@@ -166,20 +156,56 @@
             device_id_type=MESH,
         )
 
-    for c in range(stages):
-        for index, (dz, ds) in enumerate(SIDES):
-            @pl.when(there(dz, ds))
+    def blur_columns(z, carry):
+        for h in range(rows // 8):
+            cells = [vol[t, pl.ds(8 * h * slabs + z, 8, stride=slabs), :] for t in range(tiles)]
+            nothing = jnp.zeros_like(cells[0])
+            for t in range(tiles):
+                before = cells[t - 1] if t > 0 else nothing
+                after = cells[t + 1] if t < tiles - 1 else nothing
+                ext_field[t, z + 2, EDGE + 8 * h:EDGE + 8 * h + 8] = (
+                    next_lane(cells[t], after, lane8)
+                    + previous_lane(cells[t], before, lane8)
+                    + 2.0 * cells[t]
+                )
+        return carry
+
+    def start_halos(chosen):
+        for c in range(stages):
+            for index in chosen:
+                dz, ds = SIDES[index]
+
+                @pl.when(there(dz, ds))
+                def _(c=c, index=index):
+                    halo(c, index, True).start()
+
+    def wait_halos(c, chosen):
+        for index in chosen:
+            dz, ds = SIDES[index]
+
+            @pl.when(there(-dz, -ds))
             def _(c=c, index=index):
-                halo(c, index, True).start()
+                halo(c, index, False).wait_recv()
+
+    over_depth = [i for i, (dz, _) in enumerate(SIDES) if dz != 0]
+    over_strip = [i for i, (dz, _) in enumerate(SIDES) if dz == 0]
+    lax.fori_loop(0, 2, blur_columns, 0)
+    lax.fori_loop(slabs - 2, slabs, blur_columns, 0)
+    pl.semaphore_wait(barrier, expected)
+    start_halos(over_depth)
+    lax.fori_loop(2, slabs - 2, blur_columns, 0)
+    start_halos(over_strip)
 
     row = lax.broadcasted_iota(jnp.int32, (tall, LANES), 0)
     inside = ((row > 0) | (strip > 0)) & ((row != rows + 1) | (strip < strips - 1))
     scale = jnp.where(inside, 1.0 / 64.0, 0.0)
     scale_front = jnp.where(inside & (depth > 0), 1.0 / 64.0, 0.0)
     scale_back = jnp.where(inside & (depth < groups - 1), 1.0 / 64.0, 0.0)
+    for scalar in scalars:
+        scalar.wait()
     light = [light_ref[0] / 32.0, light_ref[1] / 32.0, light_ref[2] / 32.0]
 
-    def gradients(t, carry):
+    def smooth_slices(t, low, high):
         def over_rows(z):
             return (
                 ext_field[t, z, EDGE - 2:EDGE - 2 + tall]
@@ -187,44 +213,42 @@
                 + 2.0 * ext_field[t, z, EDGE - 1:EDGE - 1 + tall]
             )
 
-        one, two = over_rows(0), over_rows(1)
-        for z in range(slabs + 2):
+        one, two = over_rows(low), over_rows(low + 1)
+        for z in range(low, high):
             three = over_rows(z + 2)
             weight = scale_front if z == 0 else scale_back if z == slabs + 1 else scale
             smooth[t, z] = jnp.where(weight > 0.0, (one + three + 2.0 * two) * weight, 0.0)
             one, two = two, three
 
+    def gradients(t, low, high):
         def rows_of(z):
-            low = smooth[t, z, 0:rows]
+            under = smooth[t, z, 0:rows]
             middle = smooth[t, z, 1:rows + 1]
-            high = smooth[t, z, 2:rows + 2]
-            return low + high + 2.0 * middle, high - low
-
-        sums, slopes = zip(*[rows_of(0), rows_of(1)])
-        sums, slopes = list(sums), list(slopes)
-        for z in range(slabs):
-            more, steeper = rows_of(z + 2)
-            sums.append(more)
-            slopes.append(steeper)
+            over = smooth[t, z, 2:rows + 2]
+            return under + over + 2.0 * middle, over - under
+
+        one, two = rows_of(low), rows_of(low + 1)
+        for z in range(low, high):
+            three = rows_of(z + 2)
             across = (
-                light[0] * (slopes[z] + slopes[z + 2] + 2.0 * slopes[z + 1])
-                + light[1] * (sums[z + 2] - sums[z])
+                light[0] * (one[1] + three[1] + 2.0 * two[1])
+                + light[1] * (three[0] - one[0])
             )
-            along = light[2] * (sums[z] + sums[z + 2] + 2.0 * sums[z + 1])
+            along = light[2] * (one[0] + three[0] + 2.0 * two[0])
             ahead[t, z] = across + along
             behind[t + 1, z] = across - along
-        return carry
+            one, two = two, three
 
     extinction = ext_ref[0]
-    slope = [0.5 * color_ref[k, 0] for k in range(3)]
-    offset = [0.5 * color_ref[k, 1] for k in range(3)]
-
-    def render(t, carry):
+    slope = [0.5 * color_ref[0, k] for k in range(3)]
+    offset = [0.5 * color_ref[1, k] for k in range(3)]
+
+    def render(t, low, high):
         optical = jnp.zeros((rows, LANES), jnp.float32)
         passed = jnp.ones((rows, LANES), jnp.float32)
         total = jnp.zeros((rows, LANES), jnp.float32)
         tinted = [jnp.zeros((rows, LANES), jnp.float32) for _ in range(3)]
-        for z in range(slabs):
+        for z in range(low, high):
             up, down = ahead[t, z], behind[t + 1, z]
             facing = (
                 next_lane(up, ahead[t + 1, z], lane)
@@ -243,9 +267,36 @@
             total += weight
             for k in range(3):
                 tinted[k] += weight * jnp.tanh(slope[k] * field + offset[k])
-        for k in range(3):
-            picture[t, k] = 0.5 * (total + tinted[k])
-        picture[t, 3] = passed
+        return [0.5 * (total + tinted[k]) for k in range(3)] + [passed]
+
+    def over(front, back):
+        return [front[k] + front[3] * back[k] for k in range(3)] + [front[3] * back[3]]
+
+    inner = (2, max(2, slabs - 2))
+
+    def inner_field(t, carry):
+        smooth_slices(t, inner[0], inner[1] + 2)
+        gradients(t, *inner)
+        return carry
+
+    def inner_render(t, carry):
+        value = render(t, *inner)
+        for k in range(4):
+            picture[t, k] = value[k]
+        return carry
+
+    def outer_field(t, carry):
+        smooth_slices(t, 0, inner[0])
+        smooth_slices(t, inner[1] + 2, slabs + 2)
+        gradients(t, 0, inner[0])
+        gradients(t, inner[1], slabs)
+        return carry
+
+    def outer_render(t, carry):
+        value = over(render(t, 0, inner[0]), [picture[t, k] for k in range(4)])
+        value = over(value, render(t, inner[1], slabs))
+        for k in range(4):
+            picture[t, k] = value[k]
         return carry
 
     def swap(level, step, part, sender):
@@ -298,13 +349,14 @@
                     )
 
     for c in range(stages):
-        for index, (dz, ds) in enumerate(SIDES):
-            @pl.when(there(-dz, -ds))
-            def _(c=c, index=index):
-                halo(c, index, False).wait_recv()
-
-        lax.fori_loop(starts[c], ends[c], gradients, 0)
-        lax.fori_loop(c * per_stage, (c + 1) * per_stage, render, 0)
+        wait_halos(c, over_strip)
+    lax.fori_loop(0, tiles, inner_field, 0)
+    lax.fori_loop(0, tiles, inner_render, 0)
+
+    for c in range(stages):
+        wait_halos(c, over_depth)
+        lax.fori_loop(starts[c], ends[c], outer_field, 0)
+        lax.fori_loop(c * per_stage, (c + 1) * per_stage, outer_render, 0)
         fill(0, c, lambda k, t: picture[t, k])
         dispatch(0, c)
 
@@ -328,9 +380,7 @@
 
             value = [channel(0, k) for k in range(4)]
             for j in range(1, radix):
-                value = [value[k] + value[3] * channel(j, k) for k in range(3)] + [
-                    value[3] * channel(j, 3)
-                ]
+                value = over(value, [channel(j, k) for k in range(4)])
             merged.append(value)
         current = merged
 
@@ -363,9 +413,12 @@
     image = pl.pallas_call(
         functools.partial(kernel, groups, strips, rows, slabs, columns),
         out_shape=jax.ShapeDtypeStruct((4, rows, block), f32),
-        in_specs=[pl.BlockSpec(memory_space=pltpu.SMEM)] * 3 + [pl.BlockSpec(memory_space=pl.ANY)],
+        in_specs=[pl.BlockSpec(memory_space=pl.ANY)] * 4,
         out_specs=pl.BlockSpec(memory_space=pltpu.VMEM),
         scratch_shapes=[
+            pltpu.SMEM((1,), f32),
+            pltpu.SMEM((2, 3), f32),
+            pltpu.SMEM((3,), f32),
             pltpu.VMEM((tiles, rows * slabs, LANES), f32),
             pltpu.VMEM((tiles, slabs + 4, rows + 2 * EDGE, LANES), f32),
             pltpu.VMEM((tiles, slabs + 2, rows + 8, LANES), f32),
@@ -375,15 +428,16 @@
             *buffers,
             *buffers,
             pltpu.SemaphoreType.DMA((tiles,)),
+            pltpu.SemaphoreType.DMA((3,)),
             pltpu.SemaphoreType.DMA((stages, len(SIDES))),
             pltpu.SemaphoreType.DMA((stages, len(SIDES))),
             pltpu.SemaphoreType.DMA((len(levels), 3, most)),
             pltpu.SemaphoreType.DMA((len(levels), 3, most)),
         ],
         compiler_params=pltpu.CompilerParams(
-            collective_id=0, has_side_effects=True, vmem_limit_bytes=32 * 1024 * 1024
+            collective_id=0, has_side_effects=True, vmem_limit_bytes=60 * 1024 * 1024
         ),
-    )(extinction, color_map, light_direction, volume.reshape(rows * slabs, columns))
+    )(extinction, color_map.T, light_direction, volume.reshape(rows * slabs, columns))
     last = lax.broadcasted_iota(jnp.int32, image.shape, 0) == 3
     return jnp.where(last, 1.0 - image, image)
 

time: 27.3 us -> 25.5 us (0.934)
  local copies, waits for them, and re-layouts: 2.46 us -> 0 us
  other arithmetic: 0.69 us -> 1.45 us
    unnamed x5 -> x0, local copies, waits for them, and re-layouts: 2.46 us -> none
    select_n x1, other arithmetic: 0.69 us -> 1.45 us  [local(): return jnp.where(last, 1.0 - image, image)]
where the time goes in v2:
time: 25.5 us; the launch traced here: 25.2 us
  Pallas kernels  23.1 us (91%)
  other arithmetic  1.45 us (6%)
  between operations  0.67 us (3%)
    pallas_call x1, Pallas kernels, local(): pl.pallas_call(functools.partial(kernel, groups, strips, rows, slabs, col...  23.1 us
    select_n x1, other arithmetic, local(): return jnp.where(last, 1.0 - image, image)  1.45 us

profile of v2, /device:TPU:0, one launch (start us, length us, event | category | flops | bytes accessed | tf_op | source)
XLA Modules:
  0.0 25.2 jit_solution(414956204588402937)
XLA Ops:
  0.7 23.1 %shard_map.46 = f32[4,16,64]{2,1,0:T(8,128)} custom-call(f32[1]{0:T(128)S(6)} %copy.5.ext_hbm, f32[2,3]{1,0:T(2,128)} %bitcast.3, f32[3]{0:T(128)} %light_hbm.1, f32[128,1024]{1,0:T(8,128)} %bitcast.2), custom_call_target="tpu_custom_call" | custom-call | tf_op jit(solution)/shard_map/pallas_call | solution.py:413
  23.8 1.4 %subtract_select_fusion = f32[4,16,64]{2,1,0:T(8,128)} fusion(f32[4,16,64]{2,1,0:T(8,128)} %shard_map.46, pred[4]{0:T(512)(128)(4,1)S(1)} %iota_compare_fusion), kind=kLoop, calls=%fused_computation | loop fusion | flops 8192 | bytes 32772 | tf_op jit(solution)/shard_map/jit(_where)/select_n | solution.py:442
  (1 shorter events, 0.0 us)

commit v3 on v2

--- a/solution.py
+++ b/solution.py
@@ -1,4 +1,5 @@
 import functools
+import math
 
 import jax
 import jax.numpy as jnp
@@ -239,12 +240,13 @@
             behind[t + 1, z] = across - along
             one, two = two, three
 
-    extinction = ext_ref[0]
+    to_double = 2.0 / math.log(2.0)
+    thinning = ext_ref[0] * (-1.0 / math.log(2.0))
     slope = [0.5 * color_ref[0, k] for k in range(3)]
     offset = [0.5 * color_ref[1, k] for k in range(3)]
 
     def render(t, low, high):
-        optical = jnp.zeros((rows, LANES), jnp.float32)
+        density = jnp.zeros((rows, LANES), jnp.float32)
         passed = jnp.ones((rows, LANES), jnp.float32)
         total = jnp.zeros((rows, LANES), jnp.float32)
         tinted = [jnp.zeros((rows, LANES), jnp.float32) for _ in range(3)]
@@ -255,14 +257,13 @@
                 + previous_lane(down, behind[t, z], lane)
                 + (up + down)
             )
-            shading = 1.0 - 0.7 * pl.reciprocal(1.0 + facing * facing)
+            stretch = 1.0 + facing * facing
+            guess = pl.reciprocal(stretch, approx=True)
+            inverse = guess * (2.0 - stretch * guess)
             field = smooth[t, z + 1, 1:rows + 1]
-            double = 2.0 * field
-            optical += extinction * (
-                jnp.maximum(double, 0.0) + jnp.log1p(jnp.exp(-jnp.abs(double)))
-            )
-            beyond = jnp.exp(-optical)
-            weight = (passed - beyond) * shading
+            density += jnp.log(1.0 + jnp.exp2(to_double * field))
+            beyond = jnp.exp2(thinning * density)
+            weight = (passed - beyond) * (1.0 - 0.7 * inverse)
             passed = beyond
             total += weight
             for k in range(3):
@@ -435,7 +436,7 @@
             pltpu.SemaphoreType.DMA((len(levels), 3, most)),
         ],
         compiler_params=pltpu.CompilerParams(
-            collective_id=0, has_side_effects=True, vmem_limit_bytes=60 * 1024 * 1024
+            collective_id=0, has_side_effects=True, vmem_limit_bytes=56 * 1024 * 1024
         ),
     )(extinction, color_map.T, light_direction, volume.reshape(rows * slabs, columns))
     last = lax.broadcasted_iota(jnp.int32, image.shape, 0) == 3

time: 25.5 us -> 25.5 us (level)
  no operation moved by 1% of the time
where the time goes in v3:
time: 25.5 us; the launch traced here: 25.2 us
  Pallas kernels  23.1 us (91%)
  other arithmetic  1.45 us (6%)
  between operations  0.67 us (3%)
    pallas_call x1, Pallas kernels, local(): pl.pallas_call(functools.partial(kernel, groups, strips, rows, slabs, col...  23.1 us
    select_n x1, other arithmetic, local(): return jnp.where(last, 1.0 - image, image)  1.45 us

profile of v3, /device:TPU:0, one launch (start us, length us, event | category | flops | bytes accessed | tf_op | source)
XLA Modules:
  0.0 25.2 jit_solution(10757792009182196364)
XLA Ops:
  0.7 23.1 %shard_map.46 = f32[4,16,64]{2,1,0:T(8,128)} custom-call(f32[1]{0:T(128)S(6)} %copy.5.ext_hbm, f32[2,3]{1,0:T(2,128)} %bitcast.3, f32[3]{0:T(128)} %light_hbm.1, f32[128,1024]{1,0:T(8,128)} %bitcast.2), custom_call_target="tpu_custom_call" | custom-call | tf_op jit(solution)/shard_map/pallas_call | solution.py:414
  23.8 1.4 %subtract_select_fusion = f32[4,16,64]{2,1,0:T(8,128)} fusion(f32[4,16,64]{2,1,0:T(8,128)} %shard_map.46, pred[4]{0:T(512)(128)(4,1)S(1)} %iota_compare_fusion), kind=kLoop, calls=%fused_computation | loop fusion | flops 8192 | bytes 32772 | tf_op jit(solution)/shard_map/jit(_where)/select_n | solution.py:443
  (1 shorter events, 0.0 us)

commit v4 on v3

--- a/solution.py
+++ b/solution.py
@@ -171,14 +171,21 @@
                 )
         return carry
 
-    def start_halos(chosen):
-        for c in range(stages):
-            for index in chosen:
-                dz, ds = SIDES[index]
-
-                @pl.when(there(dz, ds))
-                def _(c=c, index=index):
-                    halo(c, index, True).start()
+    def start_halos(c, chosen):
+        for index in chosen:
+            dz, ds = SIDES[index]
+
+            @pl.when(there(dz, ds))
+            def _(c=c, index=index):
+                halo(c, index, True).start()
+
+    def leave_halos(c, chosen):
+        for index in chosen:
+            dz, ds = SIDES[index]
+
+            @pl.when(there(dz, ds))
+            def _(c=c, index=index):
+                halo(c, index, True).wait_send()
 
     def wait_halos(c, chosen):
         for index in chosen:
@@ -193,9 +200,10 @@
     lax.fori_loop(0, 2, blur_columns, 0)
     lax.fori_loop(slabs - 2, slabs, blur_columns, 0)
     pl.semaphore_wait(barrier, expected)
-    start_halos(over_depth)
+    start_halos(0, over_depth)
     lax.fori_loop(2, slabs - 2, blur_columns, 0)
-    start_halos(over_strip)
+    for c in range(stages):
+        start_halos(c, over_strip)
 
     row = lax.broadcasted_iota(jnp.int32, (tall, LANES), 0)
     inside = ((row > 0) | (strip > 0)) & ((row != rows + 1) | (strip < strips - 1))
@@ -300,54 +308,55 @@
             picture[t, k] = value[k]
         return carry
 
-    def swap(level, step, part, sender):
-        digit, other, target = partner(level, step if sender else -step)
+    def swap(level, other, part, sender):
+        radix, stride, _, _ = levels[level]
+        digit = depth // stride % radix
         source, slot = (other, digit) if sender else (digit, other)
         return pltpu.make_async_remote_copy(
             src_ref=sent[level].at[source, part],
             dst_ref=got[level].at[slot, part],
-            send_sem=swap_send.at[level, step - 1, part],
-            recv_sem=swap_recv.at[level, step - 1, part],
-            device_id=(target, strip),
+            send_sem=swap_send.at[level, source, part],
+            recv_sem=swap_recv.at[level, slot, part],
+            device_id=(depth + (other - digit) * stride, strip),
             device_id_type=MESH,
         )
 
-    def dispatch(level, part):
-        radix = levels[level][0]
-        for step in range(1, radix):
-            swap(level, step, part, True).start()
-        digit = partner(level, 1)[0]
-        got[level][digit, part] = sent[level][digit, part]
-
-    def fill(level, part, tile_of):
-        radix, _, held, width = levels[level]
-        per, count = piece_tiles(width)
-        for j in range(radix):
-            blocks = [q * radix + j for q in range(width // block)]
-            if width >= LANES:
-                each = LANES // block
-                blocks = blocks[part * each:(part + 1) * each]
-                for k in range(4):
-                    sent[level][j, part, k] = place(
-                        [
-                            (tile_of(k, b * block // LANES), b * block % LANES, i * block, block)
-                            for i, b in enumerate(blocks)
-                        ],
-                        lane,
+    def dispatch(level, j, part):
+        radix, stride, _, _ = levels[level]
+        digit = depth // stride % radix
+
+        @pl.when(digit != j)
+        def _():
+            swap(level, j, part, True).start()
+
+        @pl.when(digit == j)
+        def _():
+            got[level][j, part] = sent[level][j, part]
+
+    def blocks_of(level, j, part):
+        radix, _, _, width = levels[level]
+        blocks = [q * radix + j for q in range(width // block)]
+        if width >= LANES:
+            each = LANES // block
+            blocks = blocks[part * each:(part + 1) * each]
+        return blocks
+
+    def fill(level, j, part, tile_of):
+        width = levels[level][3]
+        per, _ = piece_tiles(width)
+        count = -(-4 // per)
+        for c in range(count):
+            sent[level][j, part, c] = place(
+                [
+                    (
+                        tile_of(k, b * block // LANES), b * block % LANES,
+                        (k - c * per) * width % LANES + i * block, block,
                     )
-            else:
-                for c in range(count):
-                    sent[level][j, part, c] = place(
-                        [
-                            (
-                                tile_of(k, b * block // LANES), b * block % LANES,
-                                (k - c * per) * width + i * block, block,
-                            )
-                            for k in range(c * per, min(4, (c + 1) * per))
-                            for i, b in enumerate(blocks)
-                        ],
-                        lane,
-                    )
+                    for k in range(c * per, min(4, (c + 1) * per))
+                    for i, b in enumerate(blocks_of(level, j, part))
+                ],
+                lane,
+            )
 
     for c in range(stages):
         wait_halos(c, over_strip)
@@ -355,24 +364,24 @@
     lax.fori_loop(0, tiles, inner_render, 0)
 
     for c in range(stages):
+        leave_halos(c, over_depth)
+        if c + 1 < stages:
+            start_halos(c + 1, over_depth)
         wait_halos(c, over_depth)
         lax.fori_loop(starts[c], ends[c], outer_field, 0)
         lax.fori_loop(c * per_stage, (c + 1) * per_stage, outer_render, 0)
-        fill(0, c, lambda k, t: picture[t, k])
-        dispatch(0, c)
-
-    current = None
-    for level, (radix, _, held, width) in enumerate(levels):
-        parts = max(1, width // LANES)
-        if level > 0:
-            for part in range(parts):
-                fill(level, part, lambda k, t: current[t][k])
-                dispatch(level, part)
+        for j in range(first[0]):
+            fill(0, j, c, lambda k, t: picture[t, k])
+            dispatch(0, j, c)
+
+    current = []
+    for level, (radix, stride, held, width) in enumerate(levels):
         per, _ = piece_tiles(width)
-        merged = []
-        for part in range(parts):
+        digit = depth // stride % radix
+        current, gone = [], set()
+        for part in range(max(1, width // LANES)):
             for step in range(1, radix):
-                swap(level, step, part, False).wait_recv()
+                swap(level, (digit + step) % radix, part, False).wait_recv()
 
             def channel(j, k):
                 tile = got[level][j, part, k // per]
@@ -382,21 +391,27 @@
             value = [channel(0, k) for k in range(4)]
             for j in range(1, radix):
                 value = over(value, [channel(j, k) for k in range(4)])
-            merged.append(value)
-        current = merged
+            current.append(value)
+            if level + 1 < len(levels):
+                following, _, _, narrower = levels[level + 1]
+                for j in range(following):
+                    for later in range(max(1, narrower // LANES)):
+                        needed = {b * block // LANES for b in blocks_of(level + 1, j, later)}
+                        if (j, later) not in gone and max(needed) <= part:
+                            gone.add((j, later))
+                            fill(level + 1, j, later, lambda k, t: current[t][k])
+                            dispatch(level + 1, j, later)
 
     for k in range(4):
         out_ref[k] = current[0][k][:, :block]
 
     for c in range(stages):
-        for index, (dz, ds) in enumerate(SIDES):
-            @pl.when(there(dz, ds))
-            def _(c=c, index=index):
-                halo(c, index, True).wait_send()
-    for level, (radix, _, _, width) in enumerate(levels):
+        leave_halos(c, over_strip)
+    for level, (radix, stride, _, width) in enumerate(levels):
+        digit = depth // stride % radix
         for part in range(max(1, width // LANES)):
             for step in range(1, radix):
-                swap(level, step, part, True).wait_send()
+                swap(level, (digit + step) % radix, part, True).wait_send()
 
 
 def local(volume, extinction, color_map, light_direction):
@@ -432,8 +447,8 @@
             pltpu.SemaphoreType.DMA((3,)),
             pltpu.SemaphoreType.DMA((stages, len(SIDES))),
             pltpu.SemaphoreType.DMA((stages, len(SIDES))),
-            pltpu.SemaphoreType.DMA((len(levels), 3, most)),
-            pltpu.SemaphoreType.DMA((len(levels), 3, most)),
+            pltpu.SemaphoreType.DMA((len(levels), 4, most)),
+            pltpu.SemaphoreType.DMA((len(levels), 4, most)),
         ],
         compiler_params=pltpu.CompilerParams(
             collective_id=0, has_side_effects=True, vmem_limit_bytes=56 * 1024 * 1024

time: 25.5 us -> 23.6 us (0.925)
  Pallas kernels: 23.1 us -> 21.2 us
    pallas_call x1, Pallas kernels: 23.1 us -> 21.2 us  [local(): pl.pallas_call(functools.partial(kernel, groups, strips, rows, slabs, col...]
where the time goes in v4:
time: 23.6 us; the launch traced here: 23.3 us
  Pallas kernels  21.2 us (90%)
  other arithmetic  1.45 us (6%)
  between operations  0.67 us (3%)
    pallas_call x1, Pallas kernels, local(): pl.pallas_call(functools.partial(kernel, groups, strips, rows, slabs, col...  21.2 us
    select_n x1, other arithmetic, local(): return jnp.where(last, 1.0 - image, image)  1.45 us

profile of v4, /device:TPU:0, one launch (start us, length us, event | category | flops | bytes accessed | tf_op | source)
XLA Modules:
  0.0 23.3 jit_solution(665337676210198112)
XLA Ops:
  0.7 21.2 %shard_map.46 = f32[4,16,64]{2,1,0:T(8,128)} custom-call(f32[1]{0:T(128)S(6)} %copy.5.ext_hbm, f32[2,3]{1,0:T(2,128)} %bitcast.3, f32[3]{0:T(128)} %light_hbm.1, f32[128,1024]{1,0:T(8,128)} %bitcast.2), custom_call_target="tpu_custom_call" | custom-call | tf_op jit(solution)/shard_map/pallas_call | solution.py:429
  21.9 1.4 %subtract_select_fusion = f32[4,16,64]{2,1,0:T(8,128)} fusion(f32[4,16,64]{2,1,0:T(8,128)} %shard_map.46, pred[4]{0:T(512)(128)(4,1)S(1)} %iota_compare_fusion), kind=kLoop, calls=%fused_computation | loop fusion | flops 8192 | bytes 32772 | tf_op jit(solution)/shard_map/jit(_where)/select_n | solution.py:458
  (1 shorter events, 0.0 us)

commit v5 on v4

--- a/solution.py
+++ b/solution.py
@@ -43,19 +43,25 @@
     return result
 
 
+def stages_of(groups, columns):
+    return max(1, min(columns // LANES // 2, columns // (radices_of(groups)[0] * columns // groups)))
+
+
 def plan(groups, columns):
     levels, stride, held = [], 1, columns
     for radix in radices_of(groups):
-        levels.append((radix, stride, held, held // radix))
+        width = held // radix
+        part = min(width, LANES)
+        if not levels:
+            part = min(part, width // stages_of(groups, columns))
+        levels.append((radix, stride, width, part, width // part))
         stride *= radix
-        held //= radix
+        held = width
     return levels
 
 
-def piece_tiles(width):
-    if width >= LANES:
-        return 1, 4 * (width // LANES)
-    per = min(4, LANES // width)
+def packing(part):
+    per = min(4, LANES // part)
     return per, -(-4 // per)
 
 
@@ -90,12 +96,6 @@
     def there(dz, ds):
         return (depth + dz >= 0) & (depth + dz < groups) & (strip + ds >= 0) & (strip + ds < strips)
 
-    def partner(level, step):
-        radix, stride, _, _ = levels[level]
-        digit = depth // stride % radix
-        other = (digit + step) % radix
-        return digit, other, depth + (other - digit) * stride
-
     barrier = pltpu.get_barrier_semaphore()
     expected = 0
     for dz, ds in SIDES:
@@ -105,11 +105,11 @@
         def _(dz=dz, ds=ds):
             pl.semaphore_signal(barrier, inc=1, device_id=(depth + dz, strip + ds), device_id_type=MESH)
 
-    for level, (radix, _, _, _) in enumerate(levels):
+    for radix, stride, _, _, _ in levels:
+        digit = depth // stride % radix
         for step in range(1, radix):
-            pl.semaphore_signal(
-                barrier, inc=1, device_id=(partner(level, step)[2], strip), device_id_type=MESH
-            )
+            other = depth + ((digit + step) % radix - digit) * stride
+            pl.semaphore_signal(barrier, inc=1, device_id=(other, strip), device_id_type=MESH)
             expected = expected + 1
 
     @pl.when(depth == 0)
@@ -135,7 +135,7 @@
         load.wait()
 
     first = levels[0]
-    stages = max(1, first[3] // LANES)
+    stages = first[4]
     per_stage = tiles // stages
     ends = [min(tiles, (c + 1) * per_stage + 1) for c in range(stages)]
     starts = [0] + ends[:-1]
@@ -309,7 +309,7 @@
         return carry
 
     def swap(level, other, part, sender):
-        radix, stride, _, _ = levels[level]
+        radix, stride = levels[level][:2]
         digit = depth // stride % radix
         source, slot = (other, digit) if sender else (digit, other)
         return pltpu.make_async_remote_copy(
@@ -322,7 +322,7 @@
         )
 
     def dispatch(level, j, part):
-        radix, stride, _, _ = levels[level]
+        radix, stride = levels[level][:2]
         digit = depth // stride % radix
 
         @pl.when(digit != j)
@@ -334,23 +334,19 @@
             got[level][j, part] = sent[level][j, part]
 
     def blocks_of(level, j, part):
-        radix, _, _, width = levels[level]
-        blocks = [q * radix + j for q in range(width // block)]
-        if width >= LANES:
-            each = LANES // block
-            blocks = blocks[part * each:(part + 1) * each]
-        return blocks
-
-    def fill(level, j, part, tile_of):
+        radix, _, _, width, _ = levels[level]
+        each = width // block
+        return [q * radix + j for q in range(part * each, (part + 1) * each)]
+
+    def fill(level, j, part, tile_of, span):
         width = levels[level][3]
-        per, _ = piece_tiles(width)
-        count = -(-4 // per)
+        per, count = packing(width)
         for c in range(count):
             sent[level][j, part, c] = place(
                 [
                     (
-                        tile_of(k, b * block // LANES), b * block % LANES,
-                        (k - c * per) * width % LANES + i * block, block,
+                        tile_of(k, b * block // span), b * block % span,
+                        (k - c * per) * width + i * block, block,
                     )
                     for k in range(c * per, min(4, (c + 1) * per))
                     for i, b in enumerate(blocks_of(level, j, part))
@@ -371,15 +367,15 @@
         lax.fori_loop(starts[c], ends[c], outer_field, 0)
         lax.fori_loop(c * per_stage, (c + 1) * per_stage, outer_render, 0)
         for j in range(first[0]):
-            fill(0, j, c, lambda k, t: picture[t, k])
+            fill(0, j, c, lambda k, t: picture[t, k], LANES)
             dispatch(0, j, c)
 
     current = []
-    for level, (radix, stride, held, width) in enumerate(levels):
-        per, _ = piece_tiles(width)
+    for level, (radix, stride, _, width, parts) in enumerate(levels):
+        per, _ = packing(width)
         digit = depth // stride % radix
         current, gone = [], set()
-        for part in range(max(1, width // LANES)):
+        for part in range(parts):
             for step in range(1, radix):
                 swap(level, (digit + step) % radix, part, False).wait_recv()
 
@@ -393,13 +389,12 @@
                 value = over(value, [channel(j, k) for k in range(4)])
             current.append(value)
             if level + 1 < len(levels):
-                following, _, _, narrower = levels[level + 1]
-                for j in range(following):
-                    for later in range(max(1, narrower // LANES)):
-                        needed = {b * block // LANES for b in blocks_of(level + 1, j, later)}
+                for j in range(levels[level + 1][0]):
+                    for later in range(levels[level + 1][4]):
+                        needed = [b * block // width for b in blocks_of(level + 1, j, later)]
                         if (j, later) not in gone and max(needed) <= part:
                             gone.add((j, later))
-                            fill(level + 1, j, later, lambda k, t: current[t][k])
+                            fill(level + 1, j, later, lambda k, t: current[t][k], width)
                             dispatch(level + 1, j, later)
 
     for k in range(4):
@@ -407,9 +402,9 @@
 
     for c in range(stages):
         leave_halos(c, over_strip)
-    for level, (radix, stride, _, width) in enumerate(levels):
+    for level, (radix, stride, _, _, parts) in enumerate(levels):
         digit = depth // stride % radix
-        for part in range(max(1, width // LANES)):
+        for part in range(parts):
             for step in range(1, radix):
                 swap(level, (digit + step) % radix, part, True).wait_send()
 
@@ -419,13 +414,12 @@
     groups, strips = lax.axis_size("depth"), lax.axis_size("strip")
     tiles, block = columns // LANES, columns // groups
     levels = plan(groups, columns)
-    stages = max(1, levels[0][3] // LANES)
+    stages = levels[0][4]
     f32 = jnp.float32
     buffers = []
-    for radix, _, _, width in levels:
-        parts = max(1, width // LANES)
-        buffers.append(pltpu.VMEM((radix, parts, piece_tiles(width)[1] // parts, rows, LANES), f32))
-    most = max(max(1, width // LANES) for _, _, _, width in levels)
+    for radix, _, _, width, parts in levels:
+        buffers.append(pltpu.VMEM((radix, parts, packing(width)[1], rows, LANES), f32))
+    most = max(level[4] for level in levels)
     image = pl.pallas_call(
         functools.partial(kernel, groups, strips, rows, slabs, columns),
         out_shape=jax.ShapeDtypeStruct((4, rows, block), f32),

time: 23.6 us -> 26.6 us (1.13)
  Pallas kernels: 21.2 us -> 24.2 us
    pallas_call x1, Pallas kernels: 21.2 us -> 24.2 us  [local(): pl.pallas_call(functools.partial(kernel, groups, strips, rows, slabs, col...]
where the time goes in v5:
time: 26.6 us; the launch traced here: 26.4 us
  Pallas kernels  24.2 us (91%)
  other arithmetic  1.45 us (5%)
  between operations  0.67 us (3%)
    pallas_call x1, Pallas kernels, local(): pl.pallas_call(functools.partial(kernel, groups, strips, rows, slabs, col...  24.2 us
    select_n x1, other arithmetic, local(): return jnp.where(last, 1.0 - image, image)  1.45 us

profile of v5, /device:TPU:0, one launch (start us, length us, event | category | flops | bytes accessed | tf_op | source)
XLA Modules:
  0.0 26.4 jit_solution(17674461580289546676)
XLA Ops:
  0.7 24.2 %shard_map.46 = f32[4,16,64]{2,1,0:T(8,128)} custom-call(f32[1]{0:T(128)S(6)} %copy.5.ext_hbm, f32[2,3]{1,0:T(2,128)} %bitcast.3, f32[3]{0:T(128)} %light_hbm.1, f32[128,1024]{1,0:T(8,128)} %bitcast.2), custom_call_target="tpu_custom_call" | custom-call | tf_op jit(solution)/shard_map/pallas_call | solution.py:423
  24.9 1.4 %subtract_select_fusion = f32[4,16,64]{2,1,0:T(8,128)} fusion(f32[4,16,64]{2,1,0:T(8,128)} %shard_map.46, pred[4]{0:T(512)(128)(4,1)S(1)} %iota_compare_fusion), kind=kLoop, calls=%fused_computation | loop fusion | flops 8192 | bytes 32772 | tf_op jit(solution)/shard_map/jit(_where)/select_n | solution.py:452
  (1 shorter events, 0.0 us)

commit v6 on v5

--- a/solution.py
+++ b/solution.py
@@ -44,7 +44,7 @@
 
 
 def stages_of(groups, columns):
-    return max(1, min(columns // LANES // 2, columns // (radices_of(groups)[0] * columns // groups)))
+    return max(1, min(columns // LANES // 4, columns // (radices_of(groups)[0] * columns // groups)))
 
 
 def plan(groups, columns):
@@ -139,10 +139,12 @@
     per_stage = tiles // stages
     ends = [min(tiles, (c + 1) * per_stage + 1) for c in range(stages)]
     starts = [0] + ends[:-1]
+    spans = [(0, ends[0] // 2), (ends[0] // 2, ends[0])] + list(zip(starts[1:], ends[1:]))
 
     def halo(c, index, sender):
         dz, ds = SIDES[index]
-        span = pl.ds(starts[c], ends[c] - starts[c])
+        low, high = spans[c] if dz != 0 else (0, tiles)
+        span = pl.ds(low, high - low)
         z_from, z_to, z_count = {
             -1: (2, slabs + 2, 2), 0: (2, 2, slabs), 1: (slabs, 0, 2)}[dz]
         r_from, r_to, r_count = {
@@ -201,9 +203,9 @@
     lax.fori_loop(slabs - 2, slabs, blur_columns, 0)
     pl.semaphore_wait(barrier, expected)
     start_halos(0, over_depth)
+    start_halos(1, over_depth)
     lax.fori_loop(2, slabs - 2, blur_columns, 0)
-    for c in range(stages):
-        start_halos(c, over_strip)
+    start_halos(0, over_strip)
 
     row = lax.broadcasted_iota(jnp.int32, (tall, LANES), 0)
     inside = ((row > 0) | (strip > 0)) & ((row != rows + 1) | (strip < strips - 1))
@@ -354,16 +356,17 @@
                 lane,
             )
 
-    for c in range(stages):
-        wait_halos(c, over_strip)
+    wait_halos(0, over_strip)
     lax.fori_loop(0, tiles, inner_field, 0)
     lax.fori_loop(0, tiles, inner_render, 0)
 
     for c in range(stages):
         leave_halos(c, over_depth)
-        if c + 1 < stages:
-            start_halos(c + 1, over_depth)
-        wait_halos(c, over_depth)
+        if c + 2 < len(spans):
+            start_halos(c + 2, over_depth)
+        if c == 0:
+            wait_halos(0, over_depth)
+        wait_halos(c + 1, over_depth)
         lax.fori_loop(starts[c], ends[c], outer_field, 0)
         lax.fori_loop(c * per_stage, (c + 1) * per_stage, outer_render, 0)
         for j in range(first[0]):
@@ -400,8 +403,8 @@
     for k in range(4):
         out_ref[k] = current[0][k][:, :block]
 
-    for c in range(stages):
-        leave_halos(c, over_strip)
+    leave_halos(0, over_strip)
+    leave_halos(stages, over_depth)
     for level, (radix, stride, _, _, parts) in enumerate(levels):
         digit = depth // stride % radix
         for part in range(parts):
@@ -439,8 +442,8 @@
             *buffers,
             pltpu.SemaphoreType.DMA((tiles,)),
             pltpu.SemaphoreType.DMA((3,)),
-            pltpu.SemaphoreType.DMA((stages, len(SIDES))),
-            pltpu.SemaphoreType.DMA((stages, len(SIDES))),
+            pltpu.SemaphoreType.DMA((stages + 1, len(SIDES))),
+            pltpu.SemaphoreType.DMA((stages + 1, len(SIDES))),
             pltpu.SemaphoreType.DMA((len(levels), 4, most)),
             pltpu.SemaphoreType.DMA((len(levels), 4, most)),
         ],

time: 26.6 us -> 24.1 us (0.906)
  Pallas kernels: 24.2 us -> 21.8 us
    pallas_call x1, Pallas kernels: 24.2 us -> 21.8 us  [local(): pl.pallas_call(functools.partial(kernel, groups, strips, rows, slabs, col...]
where the time goes in v6:
time: 24.1 us; the launch traced here: 23.9 us
  Pallas kernels  21.8 us (90%)
  other arithmetic  1.45 us (6%)
  between operations  0.67 us (3%)
    pallas_call x1, Pallas kernels, local(): pl.pallas_call(functools.partial(kernel, groups, strips, rows, slabs, col...  21.8 us
    select_n x1, other arithmetic, local(): return jnp.where(last, 1.0 - image, image)  1.45 us

profile of v6, /device:TPU:0, one launch (start us, length us, event | category | flops | bytes accessed | tf_op | source)
XLA Modules:
  0.0 23.9 jit_solution(1502729581120007225)
XLA Ops:
  0.7 21.8 %shard_map.46 = f32[4,16,64]{2,1,0:T(8,128)} custom-call(f32[1]{0:T(128)S(6)} %copy.5.ext_hbm, f32[2,3]{1,0:T(2,128)} %bitcast.3, f32[3]{0:T(128)} %light_hbm.1, f32[128,1024]{1,0:T(8,128)} %bitcast.2), custom_call_target="tpu_custom_call" | custom-call | tf_op jit(solution)/shard_map/pallas_call | solution.py:426
  22.4 1.4 %subtract_select_fusion = f32[4,16,64]{2,1,0:T(8,128)} fusion(f32[4,16,64]{2,1,0:T(8,128)} %shard_map.46, pred[4]{0:T(512)(128)(4,1)S(1)} %iota_compare_fusion), kind=kLoop, calls=%fused_computation | loop fusion | flops 8192 | bytes 32772 | tf_op jit(solution)/shard_map/jit(_where)/select_n | solution.py:455
  (1 shorter events, 0.0 us)

commit v7 on v5

--- a/solution.py
+++ b/solution.py
@@ -44,7 +44,7 @@
 
 
 def stages_of(groups, columns):
-    return max(1, min(columns // LANES // 2, columns // (radices_of(groups)[0] * columns // groups)))
+    return max(1, min(columns // LANES // 4, columns // (radices_of(groups)[0] * columns // groups)))
 
 
 def plan(groups, columns):
@@ -142,7 +142,8 @@
 
     def halo(c, index, sender):
         dz, ds = SIDES[index]
-        span = pl.ds(starts[c], ends[c] - starts[c])
+        low, high = (starts[c], ends[c]) if ds == 0 else (0, tiles)
+        span = pl.ds(low, high - low)
         z_from, z_to, z_count = {
             -1: (2, slabs + 2, 2), 0: (2, 2, slabs), 1: (slabs, 0, 2)}[dz]
         r_from, r_to, r_count = {
@@ -195,15 +196,15 @@
             def _(c=c, index=index):
                 halo(c, index, False).wait_recv()
 
-    over_depth = [i for i, (dz, _) in enumerate(SIDES) if dz != 0]
+    straight = [i for i, (_, ds) in enumerate(SIDES) if ds == 0]
+    corners = [i for i, (dz, ds) in enumerate(SIDES) if dz != 0 and ds != 0]
     over_strip = [i for i, (dz, _) in enumerate(SIDES) if dz == 0]
     lax.fori_loop(0, 2, blur_columns, 0)
     lax.fori_loop(slabs - 2, slabs, blur_columns, 0)
     pl.semaphore_wait(barrier, expected)
-    start_halos(0, over_depth)
+    start_halos(0, straight + corners)
     lax.fori_loop(2, slabs - 2, blur_columns, 0)
-    for c in range(stages):
-        start_halos(c, over_strip)
+    start_halos(0, over_strip)
 
     row = lax.broadcasted_iota(jnp.int32, (tall, LANES), 0)
     inside = ((row > 0) | (strip > 0)) & ((row != rows + 1) | (strip < strips - 1))
@@ -354,16 +355,15 @@
                 lane,
             )
 
-    for c in range(stages):
-        wait_halos(c, over_strip)
+    wait_halos(0, over_strip)
     lax.fori_loop(0, tiles, inner_field, 0)
     lax.fori_loop(0, tiles, inner_render, 0)
 
     for c in range(stages):
-        leave_halos(c, over_depth)
+        leave_halos(c, straight)
         if c + 1 < stages:
-            start_halos(c + 1, over_depth)
-        wait_halos(c, over_depth)
+            start_halos(c + 1, straight)
+        wait_halos(c, straight + corners if c == 0 else straight)
         lax.fori_loop(starts[c], ends[c], outer_field, 0)
         lax.fori_loop(c * per_stage, (c + 1) * per_stage, outer_render, 0)
         for j in range(first[0]):
@@ -400,8 +400,7 @@
     for k in range(4):
         out_ref[k] = current[0][k][:, :block]
 
-    for c in range(stages):
-        leave_halos(c, over_strip)
+    leave_halos(0, over_strip + corners)
     for level, (radix, stride, _, _, parts) in enumerate(levels):
         digit = depth // stride % radix
         for part in range(parts):

time: 26.6 us -> 24.1 us (0.906)
  Pallas kernels: 24.2 us -> 21.8 us
    pallas_call x1, Pallas kernels: 24.2 us -> 21.8 us  [local(): pl.pallas_call(functools.partial(kernel, groups, strips, rows, slabs, col...]
where the time goes in v7:
time: 24.1 us; the launch traced here: 23.9 us
  Pallas kernels  21.8 us (90%)
  other arithmetic  1.45 us (6%)
  between operations  0.67 us (3%)
    pallas_call x1, Pallas kernels, local(): pl.pallas_call(functools.partial(kernel, groups, strips, rows, slabs, col...  21.8 us
    select_n x1, other arithmetic, local(): return jnp.where(last, 1.0 - image, image)  1.45 us

profile of v7, /device:TPU:0, one launch (start us, length us, event | category | flops | bytes accessed | tf_op | source)
XLA Modules:
  0.0 23.9 jit_solution(717740911821448840)
XLA Ops:
  0.7 21.8 %shard_map.46 = f32[4,16,64]{2,1,0:T(8,128)} custom-call(f32[1]{0:T(128)S(6)} %copy.5.ext_hbm, f32[2,3]{1,0:T(2,128)} %bitcast.3, f32[3]{0:T(128)} %light_hbm.1, f32[128,1024]{1,0:T(8,128)} %bitcast.2), custom_call_target="tpu_custom_call" | custom-call | tf_op jit(solution)/shard_map/pallas_call | solution.py:422
  22.5 1.4 %subtract_select_fusion = f32[4,16,64]{2,1,0:T(8,128)} fusion(f32[4,16,64]{2,1,0:T(8,128)} %shard_map.46, pred[4]{0:T(512)(128)(4,1)S(1)} %iota_compare_fusion), kind=kLoop, calls=%fused_computation | loop fusion | flops 8192 | bytes 32772 | tf_op jit(solution)/shard_map/jit(_where)/select_n | solution.py:451
  (1 shorter events, 0.0 us)

commit v8 on v4

--- a/solution.py
+++ b/solution.py
@@ -451,7 +451,7 @@
             pltpu.SemaphoreType.DMA((len(levels), 4, most)),
         ],
         compiler_params=pltpu.CompilerParams(
-            collective_id=0, has_side_effects=True, vmem_limit_bytes=56 * 1024 * 1024
+            collective_id=0, has_side_effects=True, vmem_limit_bytes=55000 * 1024
         ),
     )(extinction, color_map.T, light_direction, volume.reshape(rows * slabs, columns))
     last = lax.broadcasted_iota(jnp.int32, image.shape, 0) == 3

time: 23.6 us -> 22.8 us (0.966)
  other arithmetic: 1.45 us -> 0.69 us
  local copies, waits for them, and re-layouts: 0 us -> 0.67 us
  Pallas kernels: 21.2 us -> 20.6 us
    select_n x1, other arithmetic: 1.45 us -> 0.69 us  [local(): return jnp.where(last, 1.0 - image, image)]
    unnamed x0 -> x4, local copies, waits for them, and re-layouts: none -> 0.67 us
    pallas_call x1, Pallas kernels: 21.2 us -> 20.6 us  [local(): pl.pallas_call(functools.partial(kernel, groups, strips, rows, slabs, col...]
where the time goes in v8:
time: 22.8 us; the launch traced here: 22.6 us
  Pallas kernels  20.6 us (90%)
  other arithmetic  0.69 us (3%)
  between operations  0.68 us (3%)
  local copies, waits for them, and re-layouts  0.67 us (3%)
    pallas_call x1, Pallas kernels, local(): pl.pallas_call(functools.partial(kernel, groups, strips, rows, slabs, col...  20.6 us
    select_n x1, other arithmetic, local(): return jnp.where(last, 1.0 - image, image)  0.69 us
    unnamed x4, local copies, waits for them, and re-layouts  0.67 us

profile of v8, /device:TPU:0, one launch (start us, length us, event | category | flops | bytes accessed | tf_op | source)
XLA Modules:
  0.0 22.6 jit_solution(13213361060356156813)
XLA Ops:
  0.7 0.0 copy-start
  0.7 0.0 copy-start.1
  0.7 0.7 %copy-done = f32[3,2]{0,1:T(2,128)S(1)} copy-done((f32[3,2]{0,1:T(2,128)S(1)}, f32[3,2]{0,1:T(2,128)}, u32[]{:S(2)}) %copy-start) | copy-done | bytes 48
  1.3 0.0 copy-done.1
  1.3 20.6 %shard_map.46 = f32[4,16,64]{2,1,0:T(8,128)S(1)} custom-call(f32[1]{0:T(128)S(6)} %copy.5.ext_hbm, f32[2,3]{1,0:T(2,128)S(1)} %bitcast.2, f32[3]{0:T(128)S(1)} %copy-done.1, f32[128,1024]{1,0:T(8,128)} %bitcast.3), custom_call_target="tpu_custom_call" | custom-call | tf_op jit(solution)/shard_map/pallas_call | solution.py:429
  21.9 0.7 %subtract_select_fusion = f32[4,16,64]{2,1,0:T(8,128)} fusion(f32[4,16,64]{2,1,0:T(8,128)S(1)} %shard_map.46, pred[4]{0:T(512)(128)(4,1)S(1)} %iota_compare_fusion), kind=kLoop, calls=%fused_computation | loop fusion | flops 8192 | bytes 32772 | tf_op jit(solution)/shard_map/jit(_where)/select_n | solution.py:458
  (1 shorter events, 0.0 us)
Async XLA Ops:
  0.7 0.7 %copy-start = (f32[3,2]{0,1:T(2,128)S(1)}, f32[3,2]{0,1:T(2,128)}, u32[]{:S(2)}) copy-start(f32[3,2]{0,1:T(2,128)} %param.6) | copy-start | bytes 76
  0.7 0.7 %copy-start.1 = (f32[3]{0:T(128)S(1)}, f32[3]{0:T(128)}, u32[]{:S(2)}) copy-start(f32[3]{0:T(128)} %light_hbm.1) | copy-start | bytes 40
